TPU v7x, 128 devices: a whole 4x4x4 slice. The times are simulated.
128 devices in a mesh: boson: 16 (over x, y), row: 8 (over z, core).
Axes of the slice: x: 4, y: 4, z: 4, core: 2. Of those that a mesh axis runs over, the one named last changes fastest.
Arguments:
- vertex: bfloat16 [256, 1024, 1024], P('boson', 'row'), may hold values from -6 to 6
- bubble: float32 [256, 1024], P('boson'), may hold values from 0.004 to 0.04
- vertex_cross: bfloat16 [256, 1024, 1024], P('boson', 'row'), may hold values from -6 to 6
- crossing: int32 [256, 8], P('boson', 'row'), may hold values from 0 to 255, as said below
Outputs:
- ladder: bfloat16 [256, 1024, 1024], P('boson', 'row')
- crossed: bfloat16 [256, 1024, 1024], P('boson', 'row')
Inputs may be any that keep to these rules, and one draw needn't show every extreme that they name: `crossing`: for each momentum block, the 16 bosonic indices of one aligned group send to the indices of any one aligned group of 16 either no block or exactly 2 blocks.
All inputs are finite; a program needn't handle non-finite values.
Results may differ from a plain program's by a relative error of at most 0.0075.
Values may be sent and summed in bfloat16 or wider, within the bound.
No kernel may reach another device: no remote copies, remote signals or barrier semaphores. Data moves between devices by JAX's collectives and lax.ppermute only.
A program may use at most 128 MiB of HBM per device.

v0:
```python
import jax
import jax.numpy as jnp
from jax import lax
from jax.sharding import PartitionSpec as P

CAP = 2
ITERS = 6


def sweeps(matrices, scales, start_rows):

    def one_index(triple):
        matrix, factor, first = triple
        start = first.astype(jnp.float32)
        current = start
        for iteration in range(ITERS):
            scaled = (current * factor[None, :]).astype(jnp.bfloat16)
            current = start + jnp.dot(scaled, matrix, preferred_element_type=jnp.float32)
        return current.astype(jnp.bfloat16)

    return lax.map(one_index, (matrices, scales, start_rows))


def local(vertex, bubble, vertex_cross, crossing):
    n_boson = lax.axis_size("boson")
    q_local = vertex.shape[0]
    row_count = vertex.shape[1]
    width = vertex.shape[2]
    gathered = lax.all_gather(vertex, "row", axis=1, tiled=True)
    ladder = sweeps(gathered, bubble, vertex)
    blocks_dev = crossing.shape[1]
    freq_rows = row_count // blocks_dev
    slots = n_boson * CAP
    data = ladder.reshape(q_local, blocks_dev, freq_rows, width)
    target_dev = crossing // q_local
    target_local = crossing % q_local
    source_iota = lax.broadcasted_iota(jnp.int32, (q_local, q_local, blocks_dev), 0)
    other_iota = lax.broadcasted_iota(jnp.int32, (q_local, q_local, blocks_dev), 1)
    same_dev = (target_dev[:, None, :] == target_dev[None, :, :]) & (other_iota < source_iota)
    position = jnp.sum(same_dev.astype(jnp.int32), axis=1)
    slot_of = target_dev * CAP + position
    slot_iota = lax.broadcasted_iota(jnp.int32, (slots, q_local, blocks_dev), 0)
    matches = slot_of[None, :, :] == slot_iota
    selector = matches.astype(jnp.bfloat16)
    outgoing = jnp.einsum(
        "sjk,jkfm->skfm", selector, data, preferred_element_type=jnp.float32
    ).astype(jnp.bfloat16)
    target_ids = jnp.max(jnp.where(matches, target_local[None, :, :], -1), axis=1)
    outgoing = outgoing.reshape(n_boson, CAP, blocks_dev, freq_rows, width)
    target_ids = target_ids.reshape(n_boson, CAP, blocks_dev)
    incoming, incoming_ids = (
        lax.all_to_all(outgoing, "boson", split_axis=0, concat_axis=0, tiled=True),
        lax.all_to_all(target_ids, "boson", split_axis=0, concat_axis=0, tiled=True),
    )
    incoming = incoming.reshape(slots, blocks_dev, freq_rows, width)
    incoming_ids = incoming_ids.reshape(slots, blocks_dev)
    owner_iota = lax.broadcasted_iota(jnp.int32, (q_local, slots, blocks_dev), 0)
    collect = (incoming_ids[None, :, :] == owner_iota).astype(jnp.bfloat16)
    summed = jnp.einsum("tsk,skfm->tkfm", collect, incoming, preferred_element_type=jnp.float32)
    other = vertex_cross.reshape(q_local, blocks_dev, freq_rows, width).astype(jnp.float32)
    crossed = (other + summed).astype(jnp.bfloat16).reshape(q_local, row_count, width)
    return (ladder, crossed)


def solution(mesh):
    placed = (P("boson", "row", None), P("boson", None), P("boson", "row", None), P("boson", "row"))
    return jax.shard_map(
        local,
        mesh=mesh,
        in_specs=placed,
        out_specs=(P("boson", "row", None), P("boson", "row", None)),
        check_vma=False,
    )
```

profile of v0, /device:TPU:20, one launch (start us, length us, event | category | flops | bytes accessed | tf_op | source)
XLA Modules:
  0.0 572.5 jit_solution(17438364384861663725)
XLA Ops:
  8.9 7.2 %all-to-all-start.1 = ((s32[16,2,1]{1,2,0:T(1,128)}), s32[16,2,1]{1,2,0:T(1,128)S(1)}, u32[]{:S(2)}, u32[]{:S(2)}) async-start(s32[16,2,1]{1,2,0:T(1,128)} %bitcast.13), calls=%async_computation.1 | async-start | bytes 16384 | tf_op jit(solution)/shard_map/all_to_all | solution.py:53
  16.1 151.7 %all-gather.2.cloned.1.call-done = bf16[16,1024,1024]{2,1,0:T(8,128)(2,1)} async-done(((bf16[16,128,1024]{2,1,0:T(8,128)(2,1)}), bf16[16,1024,1024]{2,1,0:T(8,128)(2,1)}) %all-gather.2.cloned.1.call-update) | async-done | bytes 33554448 | tf_op jit(solution)/shard_map/all_gather | solution.py:29
  167.8 175.3 %while.10 = (s32[]{:T(128)}, bf16[16,128,1024]{2,1,0:T(8,128)(2,1)}, bf16[16,128,1024]{2,1,0:T(8,128)(2,1)}, f32[16,1024]{1,0:T(8,128)}, bf16[16,1024,1024]{2,1,0:T(8,128)(2,1)}, /*index=5*/s32[]{:T(128)}) while((s32[]{:T(128)}, bf16[16,128,1024]{2,1,0:T(8,128)(2,1)}, bf16[16,128,1024]{2,1,0:T(8,128)(2,1)}, f32[16,1024]{1,0:T(8,128)}, ...), condition=%wide.region_1.2_spmd, body=%wide.region_0.1_spmd.sunk | while | flops 1614020608 | bytes 15768145 | solution.py:21
  168.6 3.3 fusion.142
  175.0 3.8 fusion.144
  179.6 3.1 fusion.142
  185.8 3.8 fusion.144
  190.4 3.1 fusion.142
  196.7 3.8 fusion.144
  201.2 3.3 fusion.142
  204.6 3.2 fusion.143
  207.7 3.9 fusion.144
  212.3 3.3 fusion.142
  215.6 3.2 fusion.143
  218.8 3.9 fusion.144
  223.4 3.2 fusion.142
  229.7 3.8 fusion.144
  234.3 3.2 fusion.142
  237.5 3.1 fusion.143
  240.7 3.9 fusion.144
  245.3 3.1 fusion.142
  251.6 3.8 fusion.144
  256.1 3.4 fusion.142
  259.5 3.3 fusion.143
  262.8 4.0 fusion.144
  267.6 3.2 fusion.142
  273.9 3.8 fusion.144
  278.4 3.2 fusion.142
  284.7 3.8 fusion.144
  289.3 3.2 fusion.142
  295.7 3.8 fusion.144
  300.3 3.2 fusion.142
  306.7 3.8 fusion.144
  311.3 3.1 fusion.142
  317.5 3.8 fusion.144
  322.1 3.2 fusion.142
  328.5 3.8 fusion.144
  333.1 3.1 fusion.142
  339.3 3.8 fusion.144
  343.1 9.0 %convert_bitcast_fusion.4 = bf16[32,1,128,1024]{3,0,2,1:T(8,128)(2,1)} fusion(bf16[16,128,1024]{2,1,0:T(8,128)(2,1)} %get-tuple-element.36, s32[16]{0:T(128)S(1)} %fusion.117), kind=kOutput, calls=%fused_computation.52 | convolution fusion | flops 138412544 | bytes 12582976 | tf_op jit(solution)/shard_map/sjk,jkfm->skfm/dot_general | solution.py:45
  352.1 13.1 %reshape.254 = bf16[16,2,1,128,1024]{4,1,0,3,2:T(2,128)(2,1)} reshape(bf16[32,1,128,1024]{3,0,2,1:T(8,128)(2,1)} %convert_bitcast_fusion.4) | data formatting | bytes 16777216 | tf_op jit(solution)/shard_map/reshape | solution.py:49
  365.2 8.0 %copy.20 = bf16[16,2,1,128,1024]{4,1,3,2,0:T(2,128)(2,1)} copy(bf16[16,2,1,128,1024]{4,1,0,3,2:T(2,128)(2,1)} %reshape.254) | data formatting | bytes 16777216 | tf_op jit(solution)/shard_map/reshape | solution.py:49
  373.2 7.2 %all-to-all-start = ((bf16[16,2,1,128,1024]{4,1,3,2,0:T(2,128)(2,1)}), bf16[16,2,1,128,1024]{4,1,3,2,0:T(2,128)(2,1)}, u32[]{:S(2)}, u32[]{:S(2)}) async-start(bf16[16,2,1,128,1024]{4,1,3,2,0:T(2,128)(2,1)} %copy.20), calls=%async_computation | async-start | bytes 16777216 | tf_op jit(solution)/shard_map/all_to_all | solution.py:52
  381.7 149.8 %all-to-all-done = bf16[16,2,1,128,1024]{4,1,3,2,0:T(2,128)(2,1)} async-done(((bf16[16,2,1,128,1024]{4,1,3,2,0:T(2,128)(2,1)}), bf16[16,2,1,128,1024]{4,1,3,2,0:T(2,128)(2,1)}, u32[]{:S(2)}, u32[]{:S(2)}) %all-to-all-start) | async-done | bytes 8388640 | tf_op jit(solution)/shard_map/all_to_all | solution.py:52
  531.5 8.1 %copy.21 = bf16[16,2,1,128,1024]{4,1,0,3,2:T(2,128)(2,1)} copy(bf16[16,2,1,128,1024]{4,1,3,2,0:T(2,128)(2,1)} %all-to-all-done) | data formatting | bytes 16777216 | tf_op jit(solution)/shard_map/all_to_all | solution.py:52
  539.6 13.1 %reshape.255 = bf16[32,128,1024]{2,0,1:T(8,128)(2,1)} reshape(bf16[16,2,1,128,1024]{4,1,0,3,2:T(2,128)(2,1)} %copy.21) | data formatting | bytes 16777216 | tf_op jit(solution)/shard_map/reshape.16
  552.7 8.6 %fusion.107 = bf16[16,128,1024]{2,0,1:T(8,128)(2,1)S(1)} fusion(bf16[16,128,1024]{2,1,0:T(8,128)(2,1)} %param.8, bf16[32,128,1024]{2,0,1:T(8,128)(2,1)} %reshape.255, s32[32]{0:T(128)S(1)} %eq.90), kind=kOutput, calls=%fused_computation.53 | convolution fusion | flops 140509696 | bytes 16777344 | tf_op jit(solution)/shard_map/tsk,skfm->tkfm/dot_general | solution.py:59
  561.3 4.3 copy.23
  (42 shorter events, 52.4 us)
Async XLA Ops:
  7.2 0.7 copy-start
  7.2 160.7 %all-gather.2.cloned.1.call-start = ((), (), s32[]{:S(2)}) async-start(), calls=%async_computation.2 | async-start | bytes 37748736 | tf_op jit(solution)/shard_map/all_gather | solution.py:29
  8.9 364.3 %all-to-all-start.1 = ((s32[16,2,1]{1,2,0:T(1,128)}), s32[16,2,1]{1,2,0:T(1,128)S(1)}, u32[]{:S(2)}, u32[]{:S(2)}) async-start(s32[16,2,1]{1,2,0:T(1,128)} %bitcast.13), calls=%async_computation.1 | async-start | bytes 16384 | tf_op jit(solution)/shard_map/all_to_all | solution.py:53
  373.2 158.3 %all-to-all-start = ((bf16[16,2,1,128,1024]{4,1,3,2,0:T(2,128)(2,1)}), bf16[16,2,1,128,1024]{4,1,3,2,0:T(2,128)(2,1)}, u32[]{:S(2)}, u32[]{:S(2)}) async-start(bf16[16,2,1,128,1024]{4,1,3,2,0:T(2,128)(2,1)} %copy.20), calls=%async_computation | async-start | bytes 16777216 | tf_op jit(solution)/shard_map/all_to_all | solution.py:52
Sparse Core Ops, SparseCore 0:
  9.7 158.1 all-gather.1
where the time goes:
time: 575 us; the launch traced here: 573 us
  waiting for transfers between devices  302 us (53%)
  matrix products  180 us (31%)
  local copies, waits for them, and re-layouts  60.1 us (10%)
  starting transfers between devices  14.5 us (3%)
  between operations  14.1 us (2%)
    dot_general x48, matrix products, one_index(): jnp.dot(scaled, matrix, preferred_element_type=jnp.float32)  163 us
    all_gather x1, waiting for transfers between devices, local(): gathered = lax.all_gather(vertex, 'row', axis=1, tiled=True)  152 us
    all_to_all x1, waiting for transfers between devices, local(): lax.all_to_all(outgoing, 'boson', split_axis=0, concat_axis=0, tiled=True)  150 us
    reshape x2, local copies, waits for them, and re-layouts, local(): outgoing = outgoing.reshape(n_boson, CAP, blocks_dev, freq_rows, width)  21.1 us
    another operation x1, local copies, waits for them, and re-layouts  13.1 us
    dynamic_slice x16, local copies, waits for them, and re-layouts, sweeps(): return lax.map(one_index, (matrices, scales, start_rows))  12.2 us
  transfers between devices with their start and end apart: 3, of which 2 were waited for; matrix products, arithmetic and copies ran while one was open for 36% of the time, Pallas kernels for 0%

commit v1 on v0

v1 whole, which is shorter than its diff:
```python
import functools

import jax
import jax.numpy as jnp
from jax import lax
from jax.experimental import pallas as pl
from jax.experimental.pallas import tpu as pltpu
from jax.sharding import PartitionSpec as P

CAP = 2
ITERS = 6
GROUP = 256


def sweep_kernel(vertex_ref, bubble_ref, ladder_ref):
    blocks, _, freq, width = vertex_ref.shape
    order = blocks * freq
    per_group = GROUP // freq
    scales = bubble_ref[0]

    @pl.loop(0, blocks // per_group)
    def _(group):
        rows = pl.ds(group * per_group, per_group)
        start = vertex_ref[rows, 0].reshape(GROUP, width).astype(jnp.float32)
        current = start
        for _ in range(ITERS):
            scaled = (current * scales).astype(jnp.bfloat16)
            matrix = vertex_ref[:, 0].reshape(order, width)
            current = start + jnp.dot(scaled, matrix, preferred_element_type=jnp.float32)
        ladder_ref[rows, 0] = current.astype(jnp.bfloat16).reshape(per_group, freq, width)


def sweeps(vertex, bubble):
    blocks, count, freq, width = vertex.shape
    block = pl.BlockSpec((blocks, 1, freq, width), lambda i: (0, i, 0, 0))
    return pl.pallas_call(
        sweep_kernel,
        grid=(count,),
        in_specs=[block, pl.BlockSpec((1, 1, width), lambda i: (i, 0, 0))],
        out_specs=block,
        out_shape=jax.ShapeDtypeStruct(vertex.shape, jnp.bfloat16),
        compiler_params=pltpu.CompilerParams(vmem_limit_bytes=48 << 20),
        cost_estimate=pl.CostEstimate(
            flops=2 * ITERS * count * width**3, bytes_accessed=8 * count * width**2, transcendentals=0
        ),
        name="sweeps",
    )(vertex, bubble.reshape(count, 1, width))


def pack_kernel(crossing_ref, ladder_ref, out_ref, used, sems):
    q_local = ladder_ref.shape[0]
    for slot in range(q_local):
        used[slot] = 0
    copies = []
    for index in range(q_local):
        target = crossing_ref[index] // q_local
        position = used[target]
        used[target] = position + 1
        copy = pltpu.make_async_copy(
            ladder_ref.at[index], out_ref.at[target * CAP + position], sems.at[index]
        )
        copy.start()
        copies.append(copy)
    for copy in copies:
        copy.wait()


def pack(crossing, ladder, slots):
    q_local, freq, width = ladder.shape
    return pl.pallas_call(
        pack_kernel,
        in_specs=[pl.BlockSpec(memory_space=pltpu.SMEM), pl.BlockSpec(memory_space=pl.ANY)],
        out_specs=pl.BlockSpec(memory_space=pl.ANY),
        out_shape=jax.ShapeDtypeStruct((slots, freq, width), jnp.bfloat16),
        scratch_shapes=[pltpu.SMEM((q_local,), jnp.int32), pltpu.SemaphoreType.DMA((q_local,))],
        name="pack",
    )(crossing, ladder)


def collect_kernel(ids_ref, incoming_ref, other_ref, out_ref, total):
    slots = incoming_ref.shape[0]
    total[...] = other_ref[...].astype(jnp.float32)

    @pl.loop(0, slots)
    def _(slot):
        target = ids_ref[slot]

        @pl.when(target >= 0)
        def _():
            total[target] += incoming_ref[slot].astype(jnp.float32)

    out_ref[...] = total[...].astype(jnp.bfloat16)


def collect(ids, incoming, other, step=16):
    slots, freq, width = incoming.shape
    q_local = other.shape[0]
    block = pl.BlockSpec((q_local, step, width), lambda i: (0, i, 0))
    return pl.pallas_call(
        collect_kernel,
        grid=(freq // step,),
        in_specs=[
            pl.BlockSpec(memory_space=pltpu.SMEM),
            pl.BlockSpec((slots, step, width), lambda i: (0, i, 0)),
            block,
        ],
        out_specs=block,
        out_shape=jax.ShapeDtypeStruct(other.shape, jnp.bfloat16),
        scratch_shapes=[pltpu.VMEM((q_local, step, width), jnp.float32)],
        compiler_params=pltpu.CompilerParams(vmem_limit_bytes=32 << 20),
        name="collect",
    )(ids, incoming, other)


def slot_targets(crossing, n_boson):
    q_local = crossing.shape[0]
    target_dev = crossing // q_local
    earlier = jnp.arange(q_local)[None, :] < jnp.arange(q_local)[:, None]
    position = jnp.sum((target_dev[:, None] == target_dev[None, :]) & earlier, axis=1, dtype=jnp.int32)
    slot_of = target_dev * CAP + position
    matches = slot_of[None, :] == jnp.arange(n_boson * CAP)[:, None]
    return jnp.max(jnp.where(matches, (crossing % q_local)[None, :], -1), axis=1)


def local(vertex, bubble, vertex_cross, crossing):
    n_boson, n_row = lax.axis_size("boson"), lax.axis_size("row")
    q_local, freq, width = vertex.shape
    mine = q_local // n_row
    slots = n_boson * CAP
    crossing = crossing.reshape(q_local)
    whole = lax.all_to_all(
        vertex.reshape(n_row, mine, freq, width), "row", split_axis=0, concat_axis=0, tiled=True
    )
    scales = lax.dynamic_slice_in_dim(bubble, lax.axis_index("row") * mine, mine, 0)
    solved = sweeps(whole, scales)
    ladder = lax.all_to_all(solved, "row", split_axis=0, concat_axis=0, tiled=True)
    ladder = ladder.reshape(q_local, freq, width)
    ids = slot_targets(crossing, n_boson)
    incoming_ids = lax.all_to_all(
        ids.reshape(n_boson, CAP), "boson", split_axis=0, concat_axis=0, tiled=True
    ).reshape(slots)
    outgoing = pack(crossing, ladder, slots)
    incoming = lax.all_to_all(
        outgoing.reshape(n_boson, CAP * freq, width), "boson", split_axis=0, concat_axis=0, tiled=True
    ).reshape(slots, freq, width)
    crossed = collect(incoming_ids, incoming, vertex_cross)
    return ladder, crossed


def solution(mesh):
    placed = (P("boson", "row", None), P("boson", None), P("boson", "row", None), P("boson", "row"))
    return jax.shard_map(
        local,
        mesh=mesh,
        in_specs=placed,
        out_specs=(P("boson", "row", None), P("boson", "row", None)),
        check_vma=False,
    )
```

time: 575 us -> 443 us (0.77)
  matrix products: 180 us -> 0 us
  Pallas kernels: 0 us -> 168 us
  waiting for transfers between devices: 302 us -> 234 us
  local copies, waits for them, and re-layouts: 60.1 us -> 10.3 us
  between operations: 14.1 us -> 0.73 us
  starting transfers between devices: 14.5 us -> 24.6 us
    dot_general x50 -> x0, matrix products: 180 us -> none  [the longest x48 163 us: one_index(): jnp.dot(scaled, matrix, preferred_element_type=jnp.float32)]
    pallas_call x0 -> x3, Pallas kernels: none -> 168 us  [the longest x1 129 us: pack(): pl.pallas_call(pack_kernel, in_specs=[pl.BlockSpec(memory_space=pltpu.SME...]
    all_gather x1 -> x0, waiting for transfers between devices: 152 us -> none  [local(): gathered = lax.all_gather(vertex, 'row', axis=1, tiled=True)]
    all_to_all x2 -> x4, waiting for transfers between devices: 150 us -> 234 us  [the longest x1 136 us: local(): lax.all_to_all(outgoing.reshape(n_boson, CAP * freq, width), 'boson', spl...]
    reshape x3 -> x2, local copies, waits for them, and re-layouts: 21.8 us -> 0.09 us  [the longest x1 0.08 us: local(): incoming_ids = lax.all_to_all(ids.reshape(n_boson, CAP), 'boson', split_a...]
    another operation x1 -> x0, local copies, waits for them, and re-layouts: 13.1 us -> none
    dynamic_slice x16 -> x1, local copies, waits for them, and re-layouts: 12.2 us -> 0.01 us  [local(): lax.dynamic_slice_in_dim(bubble, lax.axis_index('row') * mine, mine, 0)]
    all_to_all x2 -> x4, starting transfers between devices: 14.5 us -> 24.6 us  [the longest x1 7.24 us: local(): lax.all_to_all(outgoing.reshape(n_boson, CAP * freq, width), 'boson', spl...]
  transfers between devices with their start and end apart: 3 -> 4, of which waited for: 2 -> 3; matrix products, arithmetic and copies ran while one was open for 36% -> 0% of each run, Pallas kernels for 0% -> 29%
where the time goes in v1:
time: 443 us; the launch traced here: 439 us
  waiting for transfers between devices  234 us (53%)
  Pallas kernels  168 us (38%)
  starting transfers between devices  24.6 us (6%)
  local copies, waits for them, and re-layouts  10.3 us (2%)
    all_to_all x1, waiting for transfers between devices, local(): lax.all_to_all(outgoing.reshape(n_boson, CAP * freq, width), 'boson', spl...  136 us
    pallas_call x1, Pallas kernels, pack(): pl.pallas_call(pack_kernel, in_specs=[pl.BlockSpec(memory_space=pltpu.SME...  129 us
    all_to_all x1, waiting for transfers between devices, local(): lax.all_to_all(vertex.reshape(n_row, mine, freq, width), 'row', split_axi...  49.7 us
    all_to_all x1, waiting for transfers between devices, local(): lax.all_to_all(solved, 'row', split_axis=0, concat_axis=0, tiled=True)  48.6 us
    pallas_call x1, Pallas kernels, sweeps(): pl.pallas_call(sweep_kernel, grid=(count,), in_specs=[block, pl.BlockSpec...  29.4 us
    pallas_call x1, Pallas kernels, collect(): pl.pallas_call(collect_kernel, grid=(freq // step,), in_specs=[pl.BlockSp...  9.89 us
    unnamed x9, local copies, waits for them, and re-layouts  9.01 us
  transfers between devices with their start and end apart: 4, of which 3 were waited for; matrix products, arithmetic and copies ran while one was open for 0% of the time, Pallas kernels for 29%

profile of v1, /device:TPU:20, one launch (start us, length us, event | category | flops | bytes accessed | tf_op | source)
XLA Modules:
  0.0 438.8 jit_solution(13765650712016168688)
XLA Ops:
  0.6 0.0 copy-start
  0.6 5.5 %all-to-all-start = ((bf16[8,2,128,1024]{3,2,1,0:T(8,128)(2,1)}), bf16[8,2,128,1024]{3,2,1,0:T(8,128)(2,1)}, u32[]{:S(2)}, u32[]{:S(2)}) async-start(bf16[8,2,128,1024]{3,2,1,0:T(8,128)(2,1)} %bitcast.15), calls=%async_computation | async-start | bytes 8388608 | tf_op jit(solution)/shard_map/all_to_all | solution.py:131
  6.1 0.0 copy-done
  6.1 49.7 %all-to-all-done.vertex_ref = bf16[8,2,128,1024]{3,2,1,0:T(8,128)(2,1)} async-done(((bf16[8,2,128,1024]{3,2,1,0:T(8,128)(2,1)}), bf16[8,2,128,1024]{3,2,1,0:T(8,128)(2,1)}, u32[]{:S(2)}, u32[]{:S(2)}) %all-to-all-start) | async-done | bytes 4194336 | tf_op jit(solution)/shard_map/all_to_all | solution.py:131
  55.9 29.4 %sweeps.1 = bf16[8,2,128,1024]{3,2,1,0:T(8,128)(2,1)S(1)} custom-call(bf16[8,2,128,1024]{3,2,1,0:T(8,128)(2,1)} %all-to-all-done.vertex_ref, f32[2,1,1024]{2,1,0:T(1,128)S(1)} %reshape.93.bubble_ref), custom_call_target="tpu_custom_call" | custom-call | flops 25769803776 | bytes 16777216 | tf_op jit(solution)/shard_map/sweeps/pallas_call | solution.py:36
  85.3 0.0 copy-start.2
  85.3 2.0 copy-done.2
  87.3 0.0 copy-start.3
  87.3 4.7 %all-to-all-start.1 = ((bf16[8,2,128,1024]{3,2,1,0:T(8,128)(2,1)}), bf16[8,2,128,1024]{3,2,1,0:T(8,128)(2,1)}, u32[]{:S(2)}, u32[]{:S(2)}) async-start(bf16[8,2,128,1024]{3,2,1,0:T(8,128)(2,1)} %copy-done.2), calls=%async_computation.1 | async-start | bytes 8388608 | tf_op jit(solution)/shard_map/all_to_all | solution.py:136
  92.0 0.0 copy-done.3
  92.0 0.2 convert_reduce_fusion
  92.2 0.1 select_reduce_fusion
  92.3 0.7 all_to_all.17
  93.0 48.6 %all-to-all-done.1 = bf16[8,2,128,1024]{3,2,1,0:T(8,128)(2,1)} async-done(((bf16[8,2,128,1024]{3,2,1,0:T(8,128)(2,1)}), bf16[8,2,128,1024]{3,2,1,0:T(8,128)(2,1)}, u32[]{:S(2)}, u32[]{:S(2)}) %all-to-all-start.1) | async-done | bytes 4194336 | tf_op jit(solution)/shard_map/all_to_all | solution.py:136
  141.7 7.2 %all-to-all-start.2 = ((s32[16,1,2]{2,1,0:T(1,128)}), s32[16,1,2]{2,1,0:T(1,128)S(1)}, u32[]{:S(2)}, u32[]{:S(2)}) async-start(s32[16,1,2]{2,1,0:T(1,128)} %bitcast.4), calls=%async_computation.2 | async-start | bytes 16384 | tf_op jit(solution)/shard_map/all_to_all | solution.py:139
  148.9 129.0 %pack.1 = bf16[32,128,1024]{2,1,0:T(8,128)(2,1)} custom-call(s32[16]{0:T(128)} %bitcast.16, bf16[16,128,1024]{2,1,0:T(8,128)(2,1)} %bitcast.1.ladder_ref), custom_call_target="tpu_custom_call" | custom-call | tf_op jit(solution)/shard_map/pack/pallas_call | solution.py:70
  277.9 0.0 all-to-all-done.2
  277.9 7.2 %all-to-all-start.3 = ((bf16[16,256,1024]{2,1,0:T(8,128)(2,1)}), bf16[16,256,1024]{2,1,0:T(8,128)(2,1)}, u32[]{:S(2)}, u32[]{:S(2)}) async-start(bf16[16,256,1024]{2,1,0:T(8,128)(2,1)} %bitcast.14), calls=%async_computation.3 | async-start | bytes 16777216 | tf_op jit(solution)/shard_map/all_to_all | solution.py:143
  285.1 0.5 broadcast.114
  285.6 0.7 reduce.3
  286.3 0.1 reshape.96.ids_ref
  286.4 135.5 %all-to-all-done.3 = bf16[16,256,1024]{2,1,0:T(8,128)(2,1)} async-done(((bf16[16,256,1024]{2,1,0:T(8,128)(2,1)}), bf16[16,256,1024]{2,1,0:T(8,128)(2,1)}, u32[]{:S(2)}, u32[]{:S(2)}) %all-to-all-start.3) | async-done | bytes 8388640 | tf_op jit(solution)/shard_map/all_to_all | solution.py:143
  421.9 0.0 copy-start.1
  421.9 2.2 copy-done.1
  424.1 9.9 %collect.1 = bf16[16,128,1024]{2,1,0:T(8,128)(2,1)} custom-call(s32[32]{0:T(128)S(1)} %reshape.96.ids_ref, bf16[32,128,1024]{2,1,0:T(8,128)(2,1)} %bitcast.6.incoming_ref, bf16[16,128,1024]{2,1,0:T(8,128)(2,1)S(1)} %copy-done.1), custom_call_target="tpu_custom_call" | custom-call | tf_op jit(solution)/shard_map/collect/pallas_call | solution.py:99
  434.0 4.8 %copy.9 = bf16[16,128,1024]{2,1,0:T(8,128)(2,1)} copy(bf16[16,128,1024]{2,1,0:T(8,128)(2,1)} %bitcast.1.ladder_ref) | data formatting | bytes 8388608
  (5 shorter events, 0.0 us)
Async XLA Ops:
  0.6 5.5 %copy-start = (f32[16,1024]{1,0:T(8,128)S(1)}, f32[16,1024]{1,0:T(8,128)}, u32[]{:S(2)}) copy-start(f32[16,1024]{1,0:T(8,128)} %param.5) | copy-start | bytes 196612
  0.6 55.2 %all-to-all-start = ((bf16[8,2,128,1024]{3,2,1,0:T(8,128)(2,1)}), bf16[8,2,128,1024]{3,2,1,0:T(8,128)(2,1)}, u32[]{:S(2)}, u32[]{:S(2)}) async-start(bf16[8,2,128,1024]{3,2,1,0:T(8,128)(2,1)} %bitcast.15), calls=%async_computation | async-start | bytes 8388608 | tf_op jit(solution)/shard_map/all_to_all | solution.py:131
  85.3 2.0 copy-start.2
  87.3 4.7 %copy-start.3 = (s32[16,1]{0,1:T(1,128)S(1)}, s32[16,1]{0,1:T(1,128)}, u32[]{:S(2)}) copy-start(s32[16,1]{0,1:T(1,128)} %param.7) | copy-start | bytes 196
  87.3 54.4 %all-to-all-start.1 = ((bf16[8,2,128,1024]{3,2,1,0:T(8,128)(2,1)}), bf16[8,2,128,1024]{3,2,1,0:T(8,128)(2,1)}, u32[]{:S(2)}, u32[]{:S(2)}) async-start(bf16[8,2,128,1024]{3,2,1,0:T(8,128)(2,1)} %copy-done.2), calls=%async_computation.1 | async-start | bytes 8388608 | tf_op jit(solution)/shard_map/all_to_all | solution.py:136
  141.7 136.2 %all-to-all-start.2 = ((s32[16,1,2]{2,1,0:T(1,128)}), s32[16,1,2]{2,1,0:T(1,128)S(1)}, u32[]{:S(2)}, u32[]{:S(2)}) async-start(s32[16,1,2]{2,1,0:T(1,128)} %bitcast.4), calls=%async_computation.2 | async-start | bytes 16384 | tf_op jit(solution)/shard_map/all_to_all | solution.py:139
  277.9 144.0 %all-to-all-start.3 = ((bf16[16,256,1024]{2,1,0:T(8,128)(2,1)}), bf16[16,256,1024]{2,1,0:T(8,128)(2,1)}, u32[]{:S(2)}, u32[]{:S(2)}) async-start(bf16[16,256,1024]{2,1,0:T(8,128)(2,1)} %bitcast.14), calls=%async_computation.3 | async-start | bytes 16777216 | tf_op jit(solution)/shard_map/all_to_all | solution.py:143
  421.9 2.2 copy-start.1

commit v2 on v0

v2 whole, which is shorter than its diff:
```python
import functools

import jax
import jax.numpy as jnp
from jax import lax
from jax.experimental import pallas as pl
from jax.experimental.pallas import tpu as pltpu
from jax.sharding import PartitionSpec as P

CAP = 2
ITERS = 6
SIDE = 4
CHUNKS = (32, 48, 48)
AHEAD = 2
VMEM = pl.BlockSpec(memory_space=pltpu.VMEM)
SMEM = pl.BlockSpec(memory_space=pltpu.SMEM)
ANY = pl.BlockSpec(memory_space=pl.ANY)


def params(mib):
    return pltpu.CompilerParams(vmem_limit_bytes=mib << 20)


def cost(flops, nbytes):
    return pl.CostEstimate(flops=int(flops), bytes_accessed=int(nbytes), transcendentals=0)


def sweep_kernel(first, rows, vertex_ref, bubble_ref, ladder_ref):
    blocks, count, freq, width = vertex_ref.shape
    order = blocks * freq
    for index in range(count):
        scales = bubble_ref[index : index + 1, :]
        start = vertex_ref[:, index, first : first + rows].reshape(blocks * rows, width).astype(jnp.float32)
        current = start
        for _ in range(ITERS):
            scaled = (current * scales).astype(jnp.bfloat16)
            matrix = vertex_ref[:, index].reshape(order, width)
            current = start + jnp.dot(scaled, matrix, preferred_element_type=jnp.float32)
        ladder_ref[:, index] = current.astype(jnp.bfloat16).reshape(blocks, rows, width)


def sweeps(vertex, bubble, first, rows):
    blocks, count, freq, width = vertex.shape
    return pl.pallas_call(
        functools.partial(sweep_kernel, first, rows),
        in_specs=[VMEM, VMEM],
        out_specs=VMEM,
        out_shape=jax.ShapeDtypeStruct((blocks, count, rows, width), jnp.bfloat16),
        compiler_params=params(32),
        cost_estimate=cost(2 * ITERS * count * blocks * rows * width * width, 2 * vertex.size),
        name="sweeps",
    )(vertex, bubble)


def pack_kernel(first, rows, place_ref, crossing_ref, part_ref, *rest):
    ladder_ref, outs, used, sem = rest[-SIDE - 3], rest[-SIDE - 2 : -2], rest[-2], rest[-1]
    q_local = part_ref.shape[0]
    keep = pltpu.make_async_copy(part_ref, ladder_ref.at[:, first : first + rows], sem)
    keep.start()
    for slot in range(SIDE * SIDE * CAP):
        used[slot] = -1
    for index in range(q_local):
        target = crossing_ref[index] // q_local
        high, low = target // SIDE, target % SIDE
        swap = place_ref[2] == 1
        one = (jnp.where(swap, low, high) - place_ref[0] + SIDE) % SIDE
        two = (jnp.where(swap, high, low) - place_ref[1] + SIDE) % SIDE
        slot = (one * SIDE + two) * CAP
        slot = jnp.where(used[slot] < 0, slot, slot + 1)
        used[slot] = index
    for one in range(SIDE):
        for at in range(SIDE * CAP):
            index = used[one * SIDE * CAP + at]

            @pl.when(index >= 0)
            def _():
                outs[one][at] = part_ref[index]

    keep.wait()


def pack(place, crossing, part, ladder, first, freq):
    q_local, rows, width = part.shape
    slots = SIDE * SIDE * CAP
    whole = jax.ShapeDtypeStruct((q_local, freq, width), jnp.bfloat16)
    piece = jax.ShapeDtypeStruct((SIDE * CAP, rows, width), jnp.bfloat16)
    carried = [] if ladder is None else [ladder]
    results = pl.pallas_call(
        functools.partial(pack_kernel, first, rows),
        in_specs=[SMEM, SMEM, VMEM] + [ANY] * len(carried),
        out_specs=[ANY] + [VMEM] * SIDE,
        out_shape=[whole] + [piece] * SIDE,
        scratch_shapes=[pltpu.SMEM((slots,), jnp.int32), pltpu.SemaphoreType.DMA],
        input_output_aliases={3: 0} if carried else {},
        compiler_params=params(32),
        cost_estimate=cost(0, 8 * part.size),
        name="pack",
    )(place, crossing, part, *carried)
    return results[0], list(results[1:])


def collect_kernel(first, rows, ids_ref, other_ref, *rest):
    pieces, (out_ref, total, staged, sems) = rest[:SIDE], rest[-4:]
    window = slice(first, first + rows)
    read = pltpu.make_async_copy(other_ref.at[:, window], staged, sems.at[0])
    read.start()
    read.wait()
    total[...] = staged[...].astype(jnp.float32)
    for two in range(SIDE):
        for at in range(SIDE * CAP):
            target = ids_ref[two * SIDE * CAP + at]

            @pl.when(target >= 0)
            def _():
                total[target] += pieces[two][at].astype(jnp.float32)

    staged[...] = total[...].astype(jnp.bfloat16)
    write = pltpu.make_async_copy(staged, out_ref.at[:, window], sems.at[1])
    write.start()
    write.wait()


def collect(ids, other, pieces, crossed, first):
    q_local, freq, width = other.shape
    rows = pieces[0].shape[1]
    carried = [] if crossed is None else [crossed]
    return pl.pallas_call(
        functools.partial(collect_kernel, first, rows),
        in_specs=[SMEM, ANY] + [VMEM] * SIDE + [ANY] * len(carried),
        out_specs=ANY,
        out_shape=jax.ShapeDtypeStruct(other.shape, jnp.bfloat16),
        scratch_shapes=[
            pltpu.VMEM((q_local, rows, width), jnp.float32),
            pltpu.VMEM((q_local, rows, width), jnp.bfloat16),
            pltpu.SemaphoreType.DMA((2,)),
        ],
        input_output_aliases={2 + SIDE: 0} if carried else {},
        compiler_params=params(40),
        cost_estimate=cost(0, 16 * q_local * rows * width),
        name="collect",
    )(ids, other, *pieces, *carried)


def find_kernel(place_ref, everyone_ref, ids_ref, seen):
    q_local = everyone_ref.shape[2]
    for two in range(SIDE):
        for one in range(SIDE):
            slot = (two * SIDE + one) * CAP
            ids_ref[slot] = -1
            ids_ref[slot + 1] = -1
            seen[0] = slot

            @pl.loop(0, q_local)
            def _(index):
                value = everyone_ref[two, one, index]

                @pl.when(value // q_local == place_ref[3])
                def _():
                    ids_ref[seen[0]] = value % q_local
                    seen[0] = slot + 1


def arriving(place, crossing):
    row = jnp.stack([crossing] + [shift(crossing, step, 0) for step in range(1, SIDE)])
    everyone = jnp.stack([row] + [shift(row, step, 1) for step in range(1, SIDE)])
    return pl.pallas_call(
        find_kernel,
        in_specs=[SMEM, SMEM],
        out_specs=SMEM,
        out_shape=jax.ShapeDtypeStruct((CAP * SIDE * SIDE,), jnp.int32),
        scratch_shapes=[pltpu.SMEM((1,), jnp.int32)],
        name="find",
    )(place, everyone)


def shift(value, step, phase):
    n_row = lax.axis_size("row")
    pairs = []
    for x in range(SIDE):
        for y in range(SIDE):
            for row in range(n_row):
                if row % 2 == phase:
                    target = (x + step) % SIDE * SIDE + y
                else:
                    target = x * SIDE + (y + step) % SIDE
                pairs.append(((x * SIDE + y) * n_row + row, target * n_row + row))
    return lax.ppermute(value, ("boson", "row"), pairs)


def regroup_kernel(*refs):
    for two in range(SIDE):
        for one in range(SIDE):
            refs[SIDE + two][one * CAP : one * CAP + CAP] = refs[one][two * CAP : two * CAP + CAP]


def regroup(pieces):
    shape = jax.ShapeDtypeStruct(pieces[0].shape, pieces[0].dtype)
    return pl.pallas_call(
        regroup_kernel,
        in_specs=[VMEM] * SIDE,
        out_specs=[VMEM] * SIDE,
        out_shape=[shape] * SIDE,
        compiler_params=params(32),
        cost_estimate=cost(0, 4 * SIDE * pieces[0].size),
        name="regroup",
    )(*pieces)


def after(value, *earlier):
    return lax.optimization_barrier((value, *earlier))[0]


def spread(pieces, phase):
    moved = {step: shift(pieces[step], step, phase) for step in (1, 3, 2)}
    return [pieces[0]] + [moved[step] for step in range(1, SIDE)]


def exchange(pieces, earlier=()):
    again = regroup(spread(pieces, 0))
    if earlier:
        again, _ = lax.optimization_barrier((again, earlier))
    return spread(again, 1), again[1]


def local(vertex, bubble, vertex_cross, crossing):
    n_row = lax.axis_size("row")
    q_local, freq, width = vertex.shape
    mine = q_local // n_row
    me = lax.axis_index("boson")
    odd = lax.axis_index("row") % 2
    high, low = me // SIDE, me % SIDE
    place = jnp.stack([jnp.where(odd == 1, low, high), jnp.where(odd == 1, high, low), odd, me]).astype(jnp.int32)
    crossing = crossing.reshape(q_local)
    ids = arriving(place, crossing)
    whole = lax.all_to_all(
        vertex.reshape(n_row, mine, freq, width), "row", split_axis=0, concat_axis=0, tiled=True
    )
    scales = lax.dynamic_slice_in_dim(bubble, lax.axis_index("row") * mine, mine, 0)
    whole, scales, ids = lax.optimization_barrier((whole, scales, ids))
    ladder = None
    packed, summed, halfway = [], [], ()
    firsts = [sum(CHUNKS[:step]) for step in range(len(CHUNKS))]
    ready = {step: sweeps(whole, scales, firsts[step], rows) for step, rows in enumerate(CHUNKS)}
    for step, rows in enumerate(CHUNKS):
        first, solved = firsts[step], ready[step]
        if step >= 1:
            solved = after(solved, packed[step - 1])
        if step >= 2:
            solved, summed[step - 2] = lax.optimization_barrier((solved, summed[step - 2]))
        part = lax.all_to_all(solved, "row", split_axis=0, concat_axis=0, tiled=True)
        part = part.reshape(q_local, rows, width)
        part = after(part, *halfway)
        if step == 0:
            for other in range(1, min(AHEAD, len(CHUNKS))):
                part, ready[other] = lax.optimization_barrier((part, ready[other]))
        ladder, outgoing = pack(place, crossing, part, ladder, first, freq)
        packed.append(outgoing[1])
        pieces, half = exchange(outgoing, summed[step - 1 : step])
        halfway = (half,)
        summed.append(collect(ids, vertex_cross, pieces, summed[-1] if summed else None, first))
    return ladder, summed[-1]


def solution(mesh):
    placed = (P("boson", "row", None), P("boson", None), P("boson", "row", None), P("boson", "row"))
    return jax.shard_map(
        local,
        mesh=mesh,
        in_specs=placed,
        out_specs=(P("boson", "row", None), P("boson", "row", None)),
        check_vma=False,
    )
```

time: 575 us -> 221 us (0.38)
  waiting for transfers between devices: 302 us -> 111 us
  matrix products: 180 us -> 0 us
  Pallas kernels: 0 us -> 61.9 us
  local copies, waits for them, and re-layouts: 60.1 us -> 3.69 us
  starting transfers between devices: 14.5 us -> 41 us
  between operations: 14.1 us -> 1 us
    dot_general x50 -> x0, matrix products: 180 us -> none  [the longest x48 163 us: one_index(): jnp.dot(scaled, matrix, preferred_element_type=jnp.float32)]
    all_gather x1 -> x0, waiting for transfers between devices: 152 us -> none  [local(): gathered = lax.all_gather(vertex, 'row', axis=1, tiled=True)]
    all_to_all x2 -> x4, waiting for transfers between devices: 150 us -> 47.3 us  [the longest x1 30.9 us: local(): lax.all_to_all(vertex.reshape(n_row, mine, freq, width), 'row', split_axi...]
    ppermute x0 -> x24, waiting for transfers between devices: none -> 63.6 us  [shift(): return lax.ppermute(value, ('boson', 'row'), pairs)]
    pallas_call x0 -> x13, Pallas kernels: none -> 61.9 us  [the longest x3 36.7 us: sweeps(): pl.pallas_call(functools.partial(sweep_kernel, first, rows), in_specs=[VM...]
    ppermute x0 -> x24, starting transfers between devices: none -> 23.3 us  [shift(): return lax.ppermute(value, ('boson', 'row'), pairs)]
    reshape x3 -> x0, local copies, waits for them, and re-layouts: 21.8 us -> none  [the longest x2 21.1 us: local(): outgoing = outgoing.reshape(n_boson, CAP, blocks_dev, freq_rows, width)]
    another operation x1 -> x0, local copies, waits for them, and re-layouts: 13.1 us -> none
  transfers between devices with their start and end apart: 3 -> 28, of which waited for: 2 -> 20; matrix products, arithmetic and copies ran while one was open for 36% -> 1% of each run, Pallas kernels for 0% -> 22%
where the time goes in v2:
time: 221 us; the launch traced here: 220 us
  waiting for transfers between devices  111 us (50%)
  Pallas kernels  61.9 us (28%)
  starting transfers between devices  41 us (19%)
  local copies, waits for them, and re-layouts  3.69 us (2%)
    ppermute x24, waiting for transfers between devices, shift(): return lax.ppermute(value, ('boson', 'row'), pairs)  63.6 us
    pallas_call x3, Pallas kernels, sweeps(): pl.pallas_call(functools.partial(sweep_kernel, first, rows), in_specs=[VM...  36.7 us
    all_to_all x1, waiting for transfers between devices, local(): lax.all_to_all(vertex.reshape(n_row, mine, freq, width), 'row', split_axi...  30.9 us
    ppermute x24, starting transfers between devices, shift(): return lax.ppermute(value, ('boson', 'row'), pairs)  23.3 us
    all_to_all x3, waiting for transfers between devices, local(): lax.all_to_all(solved, 'row', split_axis=0, concat_axis=0, tiled=True)  16.4 us
    all_to_all x3, starting transfers between devices, local(): lax.all_to_all(solved, 'row', split_axis=0, concat_axis=0, tiled=True)  12.3 us
    pallas_call x3, Pallas kernels, collect(): pl.pallas_call(functools.partial(collect_kernel, first, rows), in_specs=[...  9.53 us
    pallas_call x3, Pallas kernels, pack(): pl.pallas_call(functools.partial(pack_kernel, first, rows), in_specs=[SME...  6.38 us
  transfers between devices with their start and end apart: 28, of which 20 were waited for; matrix products, arithmetic and copies ran while one was open for 1% of the time, Pallas kernels for 22%

profile of v2, /device:TPU:20, one launch (start us, length us, event | category | flops | bytes accessed | tf_op | source)
XLA Modules:
  0.0 219.7 jit_solution(9310605888802031892)
XLA Ops:
  0.7 5.5 %all-to-all-start = ((bf16[8,2,128,1024]{3,2,1,0:T(8,128)(2,1)}), bf16[8,2,128,1024]{3,2,1,0:T(8,128)(2,1)}, u32[]{:S(2)}, u32[]{:S(2)}) async-start(bf16[8,2,128,1024]{3,2,1,0:T(8,128)(2,1)} %bitcast.28), calls=%async_computation | async-start | bytes 8388608 | tf_op jit(solution)/shard_map/all_to_all | solution.py:235
  6.7 2.7 %collective-permute-start.1 = (s32[16]{0:T(128)S(1)}, s32[16]{0:T(128)S(1)}, u32[]{:S(2)}, u32[]{:S(2)}) collective-permute-start(s32[16]{0:T(128)S(1)} %bitcast.22), channel_id=1, source_target_pairs={{0,64},{1,17},{2,66},{3,19},{4,68},{5,21},{6,70},{7,23},{8,72},{9,... | collective-permute-start | bytes 200 | tf_op jit(solution)/shard_map/ppermute | solution.py:187
  9.7 2.0 collective-permute-done.1
  11.8 1.2 collective-permute-done
  13.4 2.2 collective-permute-start.3
  16.4 1.8 collective-permute-done.4
  18.2 1.2 collective-permute-done.5
  20.0 5.0 %find.1.ids_ref = s32[32]{0:T(128)} custom-call(s32[4]{0:T(128)} %pad_add_fusion.2.place_ref, s32[4,4,16]{2,1,0:T(4,128)} %pad_add_fusion.everyone_ref), custom_call_target="tpu_custom_call" | custom-call | tf_op jit(solution)/shard_map/find/pallas_call | solution.py:166
  25.0 30.9 %all-to-all-done.vertex_ref = bf16[8,2,128,1024]{3,2,1,0:T(8,128)(2,1)} async-done(((bf16[8,2,128,1024]{3,2,1,0:T(8,128)(2,1)}), bf16[8,2,128,1024]{3,2,1,0:T(8,128)(2,1)}, u32[]{:S(2)}, u32[]{:S(2)}) %all-to-all-start) | async-done | bytes 4194336 | tf_op jit(solution)/shard_map/all_to_all | solution.py:235
  55.9 9.9 %sweeps.4 = bf16[8,2,32,1024]{3,2,1,0:T(8,128)(2,1)} custom-call(bf16[8,2,128,1024]{3,2,1,0:T(8,128)(2,1)} %all-to-all-done.vertex_ref, f32[2,1024]{1,0:T(2,128)S(1)} %constant_dynamic-slice_fusion.bubble_ref), custom_call_target="tpu_custom_call" | custom-call | flops 6442450944 | bytes 4194304 | tf_op jit(solution)/shard_map/sweeps/pallas_call | solution.py:44
  65.8 3.7 %all-to-all-start.1 = ((bf16[8,2,32,1024]{3,2,1,0:T(8,128)(2,1)}), bf16[8,2,32,1024]{3,2,1,0:T(8,128)(2,1)S(1)}, u32[]{:S(2)}, u32[]{:S(2)}) async-start(bf16[8,2,32,1024]{3,2,1,0:T(8,128)(2,1)} %sweeps.4), calls=%async_computation.1 | async-start | bytes 2097152 | tf_op jit(solution)/shard_map/all_to_all | solution.py:250
  69.5 13.3 %sweeps.5 = bf16[8,2,48,1024]{3,2,1,0:T(8,128)(2,1)} custom-call(bf16[8,2,128,1024]{3,2,1,0:T(8,128)(2,1)} %all-to-all-done.vertex_ref, f32[2,1024]{1,0:T(2,128)S(1)} %constant_dynamic-slice_fusion.bubble_ref), custom_call_target="tpu_custom_call" | custom-call | flops 9663676416 | bytes 4194304 | tf_op jit(solution)/shard_map/sweeps/pallas_call | solution.py:44
  82.8 2.4 %all-to-all-done.1 = bf16[8,2,32,1024]{3,2,1,0:T(8,128)(2,1)S(1)} async-done(((bf16[8,2,32,1024]{3,2,1,0:T(8,128)(2,1)}), bf16[8,2,32,1024]{3,2,1,0:T(8,128)(2,1)S(1)}, u32[]{:S(2)}, u32[]{:S(2)}) %all-to-all-start.1) | async-done | bytes 1048608 | tf_op jit(solution)/shard_map/all_to_all | solution.py:250
  85.2 1.5 pack.3
  87.6 3.6 %all-to-all-start.2 = ((bf16[8,2,48,1024]{3,2,1,0:T(8,128)(2,1)}), bf16[8,2,48,1024]{3,2,1,0:T(8,128)(2,1)S(1)}, u32[]{:S(2)}, u32[]{:S(2)}) async-start(bf16[8,2,48,1024]{3,2,1,0:T(8,128)(2,1)} %sweeps.5), calls=%async_computation.2 | async-start | bytes 3145728 | tf_op jit(solution)/shard_map/all_to_all | solution.py:250
  91.7 2.2 collective-permute-start.8
  93.9 8.3 %collective-permute-done.7.refs_2_ = bf16[8,32,1024]{2,1,0:T(8,128)(2,1)S(1)} collective-permute-done((bf16[8,32,1024]{2,1,0:T(8,128)(2,1)}, bf16[8,32,1024]{2,1,0:T(8,128)(2,1)S(1)}, u32[]{:S(2)}, u32[]{:S(2)}) %collective-permute-start.7) | collective-permute-done | bytes 524320 | tf_op jit(solution)/shard_map/ppermute | solution.py:187
  102.2 4.6 %collective-permute-done.8.refs_3_ = bf16[8,32,1024]{2,1,0:T(8,128)(2,1)S(1)} collective-permute-done((bf16[8,32,1024]{2,1,0:T(8,128)(2,1)S(1)}, bf16[8,32,1024]{2,1,0:T(8,128)(2,1)S(1)}, u32[]{:S(2)}, u32[]{:S(2)}) %collective-permute-start.8) | collective-permute-done | bytes 524320 | tf_op jit(solution)/shard_map/ppermute | solution.py:187
  106.9 0.9 collective-permute-done.6.refs_1_
  107.7 1.3 regroup.3
  109.0 0.8 copy-done.5
  110.2 2.4 %collective-permute-start.11 = (bf16[8,32,1024]{2,1,0:T(8,128)(2,1)}, bf16[8,32,1024]{2,1,0:T(8,128)(2,1)}, u32[]{:S(2)}, u32[]{:S(2)}) collective-permute-start(bf16[8,32,1024]{2,1,0:T(8,128)(2,1)} %get-tuple-element.64), channel_id=1, source_target_pairs={{0,24},{1,97},{2,26},{3,99},{4,28},{5,101},{6,30},{7,103},{8,0},{9... | collective-permute-start | bytes 1572872 | tf_op jit(solution)/shard_map/ppermute | solution.py:187
  112.7 3.2 %pack.4 = (bf16[16,128,1024]{2,1,0:T(8,128)(2,1)}, bf16[8,48,1024]{2,1,0:T(8,128)(2,1)S(1)}, bf16[8,48,1024]{2,1,0:T(8,128)(2,1)}, bf16[8,48,1024]{2,1,0:T(8,128)(2,1)}, bf16[8,48,1024]{2,1,0:T(8,128)(2,1)}) custom-call(s32[4]{0:T(128)S(1)} %copy-done.7, s32[16]{0:T(128)S(1)} %bitcast.26, ...), custom_call_target="tpu_custom_call", output_to_operand_aliasing={{0}: (3, {})} | custom-call | bytes 6291456 | tf_op jit(solution)/shard_map/pack/pallas_call | solution.py:88
  116.5 2.1 collective-permute-start.14
  118.6 3.3 %collective-permute-done.10.rest_2_ = bf16[8,32,1024]{2,1,0:T(8,128)(2,1)} collective-permute-done((bf16[8,32,1024]{2,1,0:T(8,128)(2,1)}, bf16[8,32,1024]{2,1,0:T(8,128)(2,1)}, u32[]{:S(2)}, u32[]{:S(2)}) %collective-permute-start.10) | collective-permute-done | bytes 524320 | tf_op jit(solution)/shard_map/ppermute | solution.py:187
  122.2 13.5 %sweeps.3 = bf16[8,2,48,1024]{3,2,1,0:T(8,128)(2,1)} custom-call(bf16[8,2,128,1024]{3,2,1,0:T(8,128)(2,1)} %all-to-all-done.vertex_ref, f32[2,1024]{1,0:T(2,128)S(1)} %constant_dynamic-slice_fusion.bubble_ref), custom_call_target="tpu_custom_call" | custom-call | flops 9663676416 | bytes 4194304 | tf_op jit(solution)/shard_map/sweeps/pallas_call | solution.py:44
  135.7 2.6 %collective-permute-done.11.rest_3_ = bf16[8,32,1024]{2,1,0:T(8,128)(2,1)} collective-permute-done((bf16[8,32,1024]{2,1,0:T(8,128)(2,1)}, bf16[8,32,1024]{2,1,0:T(8,128)(2,1)}, u32[]{:S(2)}, u32[]{:S(2)}) %collective-permute-start.11) | collective-permute-done | bytes 524320 | tf_op jit(solution)/shard_map/ppermute | solution.py:187
  138.4 1.7 collective-permute-done.9.rest_1_
  140.1 3.1 %collect.3.rest_4_ = bf16[16,128,1024]{2,1,0:T(8,128)(2,1)} custom-call(s32[32]{0:T(128)S(1)} %copy-done.8, bf16[16,128,1024]{2,1,0:T(8,128)(2,1)S(1)} %copy-done.1, bf16[8,32,1024]{2,1,0:T(8,128)(2,1)S(1)} %copy-done.6, bf16[8,32,1024]{2,1,0:T(8,128)(2,1)} %collective-permute-done.9.rest_1_, bf16[8,32,1024]{2,1,0:T(8,128)(2,1)} %collective-permute-done.10.rest_2_, ...), custom_call_target="tpu_custom_call" | custom-call | bytes 8388608 | tf_op jit(solution)/shard_map/collect/pallas_call | solution.py:127
  143.2 5.0 %all-to-all-start.3 = ((bf16[8,2,48,1024]{3,2,1,0:T(8,128)(2,1)}), bf16[8,2,48,1024]{3,2,1,0:T(8,128)(2,1)S(1)}, u32[]{:S(2)}, u32[]{:S(2)}) async-start(bf16[8,2,48,1024]{3,2,1,0:T(8,128)(2,1)} %sweeps.3), calls=%async_computation.3 | async-start | bytes 3145728 | tf_op jit(solution)/shard_map/all_to_all | solution.py:250
  148.2 0.9 copy-done.3
  149.1 1.1 copy-done.4
  150.2 2.9 %regroup.4 = (bf16[8,48,1024]{2,1,0:T(8,128)(2,1)S(1)}, bf16[8,48,1024]{2,1,0:T(8,128)(2,1)}, bf16[8,48,1024]{2,1,0:T(8,128)(2,1)}, bf16[8,48,1024]{2,1,0:T(8,128)(2,1)}) custom-call(bf16[8,48,1024]{2,1,0:T(8,128)(2,1)S(1)} %get-tuple-element.66.refs_0_, bf16[8,48,1024]{2,1,0:T(8,128)(2,1)} %collective-permute-done.12.refs_1_, ...), custom_call_target="tpu_custom_call" | custom-call | bytes 6291456 | tf_op jit(solution)/shard_map/regroup/pallas_call | solution.py:198
  153.1 2.8 %collective-permute-start.20 = (bf16[8,48,1024]{2,1,0:T(8,128)(2,1)}, bf16[8,48,1024]{2,1,0:T(8,128)(2,1)}, u32[]{:S(2)}, u32[]{:S(2)}) collective-permute-start(bf16[8,48,1024]{2,1,0:T(8,128)(2,1)} %get-tuple-element.87), channel_id=1, source_target_pairs={{0,24},{1,97},{2,26},{3,99},{4,28},{5,101},{6,30},{7,103},{8,0},{9... | collective-permute-start | bytes 2359304 | tf_op jit(solution)/shard_map/ppermute | solution.py:187
  155.8 13.9 %all-to-all-done.3 = bf16[8,2,48,1024]{3,2,1,0:T(8,128)(2,1)S(1)} async-done(((bf16[8,2,48,1024]{3,2,1,0:T(8,128)(2,1)}), bf16[8,2,48,1024]{3,2,1,0:T(8,128)(2,1)S(1)}, u32[]{:S(2)}, u32[]{:S(2)}) %all-to-all-start.3) | async-done | bytes 1572896 | tf_op jit(solution)/shard_map/all_to_all | solution.py:250
  169.8 1.7 pack.5
  171.5 0.8 collective-permute-start.15
  172.3 1.1 collective-permute-start.16
  173.4 0.9 collective-permute-start.17
  174.3 2.3 %collective-permute-done.18.rest_1_ = bf16[8,48,1024]{2,1,0:T(8,128)(2,1)} collective-permute-done((bf16[8,48,1024]{2,1,0:T(8,128)(2,1)}, bf16[8,48,1024]{2,1,0:T(8,128)(2,1)}, u32[]{:S(2)}, u32[]{:S(2)}) %collective-permute-start.18) | collective-permute-done | bytes 786464 | tf_op jit(solution)/shard_map/ppermute | solution.py:187
  176.7 3.8 %collect.4.rest_4_ = bf16[16,128,1024]{2,1,0:T(8,128)(2,1)} custom-call(s32[32]{0:T(128)S(1)} %copy-done.8, bf16[16,128,1024]{2,1,0:T(8,128)(2,1)S(1)} %copy-done.2, bf16[8,48,1024]{2,1,0:T(8,128)(2,1)S(1)} %get-tuple-element.85.rest_0_, bf16[8,48,1024]{2,1,0:T(8,128)(2,1)} %collective-permute-done.18.rest_1_, ...), custom_call_target="tpu_custom_call", output_to_operand_aliasing={{}: (6, {})} | custom-call | bytes 12582912 | tf_op jit(solution)/shard_map/collect/pallas_call | solution.py:127
  180.5 11.5 %collective-permute-done.15.refs_1_ = bf16[8,48,1024]{2,1,0:T(8,128)(2,1)S(1)} collective-permute-done((bf16[8,48,1024]{2,1,0:T(8,128)(2,1)S(1)}, bf16[8,48,1024]{2,1,0:T(8,128)(2,1)S(1)}, u32[]{:S(2)}, u32[]{:S(2)}) %collective-permute-start.15) | collective-permute-done | bytes 786464 | tf_op jit(solution)/shard_map/ppermute | solution.py:187
  191.9 2.1 collective-permute-done.17.refs_3_
  194.3 1.4 collective-permute-start.21
  196.3 0.9 collective-permute-start.23
  197.2 17.5 %collective-permute-done.21.rest_1_ = bf16[8,48,1024]{2,1,0:T(8,128)(2,1)S(1)} collective-permute-done((bf16[8,48,1024]{2,1,0:T(8,128)(2,1)S(1)}, bf16[8,48,1024]{2,1,0:T(8,128)(2,1)S(1)}, u32[]{:S(2)}, u32[]{:S(2)}) %collective-permute-start.21) | collective-permute-done | bytes 786464 | tf_op jit(solution)/shard_map/ppermute | solution.py:187
  214.8 2.1 collective-permute-done.23.rest_3_
  216.9 2.7 %collect.5 = bf16[16,128,1024]{2,1,0:T(8,128)(2,1)} custom-call(s32[32]{0:T(128)S(1)} %copy-done.8, bf16[16,128,1024]{2,1,0:T(8,128)(2,1)S(1)} %copy-done.2, bf16[8,48,1024]{2,1,0:T(8,128)(2,1)S(1)} %get-tuple-element.88.rest_0_, bf16[8,48,1024]{2,1,0:T(8,128)(2,1)S(1)} %collective-permute-done.21.rest_1_, ...), custom_call_target="tpu_custom_call", output_to_operand_aliasing={{}: (6, {})} | custom-call | bytes 12582912 | tf_op jit(solution)/shard_map/collect/pallas_call | solution.py:127
  (47 shorter events, 6.5 us)
Async XLA Ops:
  0.6 8.8 %copy-start = (f32[16,1024]{1,0:T(8,128)S(1)}, f32[16,1024]{1,0:T(8,128)}, u32[]{:S(2)}) copy-start(f32[16,1024]{1,0:T(8,128)} %param.5) | copy-start | bytes 196612
  0.6 5.5 %copy-start.9 = (s32[16,1]{0,1:T(1,128)S(1)}, s32[16,1]{0,1:T(1,128)}, u32[]{:S(2)}) copy-start(s32[16,1]{0,1:T(1,128)} %param.7) | copy-start | bytes 196
  0.7 55.2 %all-to-all-start = ((bf16[8,2,128,1024]{3,2,1,0:T(8,128)(2,1)}), bf16[8,2,128,1024]{3,2,1,0:T(8,128)(2,1)}, u32[]{:S(2)}, u32[]{:S(2)}) async-start(bf16[8,2,128,1024]{3,2,1,0:T(8,128)(2,1)} %bitcast.28), calls=%async_computation | async-start | bytes 8388608 | tf_op jit(solution)/shard_map/all_to_all | solution.py:235
  6.1 3.6 %collective-permute-start.2 = (s32[16]{0:T(128)S(1)}, s32[16]{0:T(128)S(1)}, u32[]{:S(2)}, u32[]{:S(2)}) collective-permute-start(s32[16]{0:T(128)S(1)} %bitcast.21), channel_id=1, source_target_pairs={{0,96},{1,25},{2,98},{3,27},{4,100},{5,29},{6,102},{7,31},{8,104},... | collective-permute-start | bytes 200 | tf_op jit(solution)/shard_map/ppermute | solution.py:187
  6.7 5.0 %collective-permute-start.1 = (s32[16]{0:T(128)S(1)}, s32[16]{0:T(128)S(1)}, u32[]{:S(2)}, u32[]{:S(2)}) collective-permute-start(s32[16]{0:T(128)S(1)} %bitcast.22), channel_id=1, source_target_pairs={{0,64},{1,17},{2,66},{3,19},{4,68},{5,21},{6,70},{7,23},{8,72},{9,... | collective-permute-start | bytes 200 | tf_op jit(solution)/shard_map/ppermute | solution.py:187
  9.5 3.5 %collective-permute-start = (s32[16]{0:T(128)S(1)}, s32[16]{0:T(128)S(1)}, u32[]{:S(2)}, u32[]{:S(2)}) collective-permute-start(s32[16]{0:T(128)S(1)} %bitcast.23), channel_id=1, source_target_pairs={{0,32},{1,9},{2,34},{3,11},{4,36},{5,13},{6,38},{7,15},{8,40},{9,1... | collective-permute-start | bytes 200 | tf_op jit(solution)/shard_map/ppermute | solution.py:187
  13.0 5.2 %collective-permute-start.4 = (s32[4,16]{1,0:T(4,128)S(1)}, s32[4,16]{1,0:T(4,128)S(1)}, u32[]{:S(2)}, u32[]{:S(2)}) collective-permute-start(s32[4,16]{1,0:T(4,128)S(1)} %get-tuple-element.93), channel_id=1, source_target_pairs={{0,16},{1,65},{2,18},{3,67},{4,20},{5,69},{6,22},{7,71},{8,24},{9,... | collective-permute-start | bytes 776 | tf_op jit(solution)/shard_map/ppermute | solution.py:187
  13.4 4.8 %collective-permute-start.3 = (s32[4,16]{1,0:T(4,128)S(1)}, s32[4,16]{1,0:T(4,128)S(1)}, u32[]{:S(2)}, u32[]{:S(2)}) collective-permute-start(s32[4,16]{1,0:T(4,128)S(1)} %get-tuple-element.93), channel_id=1, source_target_pairs={{0,8},{1,33},{2,10},{3,35},{4,12},{5,37},{6,14},{7,39},{8,16},{9,4... | collective-permute-start | bytes 776 | tf_op jit(solution)/shard_map/ppermute | solution.py:187
  15.6 3.7 %collective-permute-start.5 = (s32[4,16]{1,0:T(4,128)S(1)}, s32[4,16]{1,0:T(4,128)S(1)}, u32[]{:S(2)}, u32[]{:S(2)}) collective-permute-start(s32[4,16]{1,0:T(4,128)S(1)} %get-tuple-element.93), channel_id=1, source_target_pairs={{0,24},{1,97},{2,26},{3,99},{4,28},{5,101},{6,30},{7,103},{8,0},{9... | collective-permute-start | bytes 776 | tf_op jit(solution)/shard_map/ppermute | solution.py:187
  65.8 19.5 %all-to-all-start.1 = ((bf16[8,2,32,1024]{3,2,1,0:T(8,128)(2,1)}), bf16[8,2,32,1024]{3,2,1,0:T(8,128)(2,1)S(1)}, u32[]{:S(2)}, u32[]{:S(2)}) async-start(bf16[8,2,32,1024]{3,2,1,0:T(8,128)(2,1)} %sweeps.4), calls=%async_computation.1 | async-start | bytes 2097152 | tf_op jit(solution)/shard_map/all_to_all | solution.py:250
  69.5 15.7 %copy-start.7 = (s32[4]{0:T(128)S(1)}, s32[4]{0:T(128)}, u32[]{:S(2)}) copy-start(s32[4]{0:T(128)} %pad_add_fusion.2.place_ref) | copy-start | bytes 52
  86.7 0.8 copy-start.10
  87.6 25.1 %all-to-all-start.2 = ((bf16[8,2,48,1024]{3,2,1,0:T(8,128)(2,1)}), bf16[8,2,48,1024]{3,2,1,0:T(8,128)(2,1)S(1)}, u32[]{:S(2)}, u32[]{:S(2)}) async-start(bf16[8,2,48,1024]{3,2,1,0:T(8,128)(2,1)} %sweeps.5), calls=%async_computation.2 | async-start | bytes 3145728 | tf_op jit(solution)/shard_map/all_to_all | solution.py:250
  91.1 11.1 %collective-permute-start.7 = (bf16[8,32,1024]{2,1,0:T(8,128)(2,1)}, bf16[8,32,1024]{2,1,0:T(8,128)(2,1)S(1)}, u32[]{:S(2)}, u32[]{:S(2)}) collective-permute-start(bf16[8,32,1024]{2,1,0:T(8,128)(2,1)} %copy-done.10), channel_id=1, source_target_pairs={{0,64},{1,17},{2,66},{3,19},{4,68},{5,21},{6,70},{7,23},{8,72},{9,... | collective-permute-start | bytes 1572872 | tf_op jit(solution)/shard_map/ppermute | solution.py:187
  91.7 15.1 %collective-permute-start.8 = (bf16[8,32,1024]{2,1,0:T(8,128)(2,1)S(1)}, bf16[8,32,1024]{2,1,0:T(8,128)(2,1)S(1)}, u32[]{:S(2)}, u32[]{:S(2)}) collective-permute-start(bf16[8,32,1024]{2,1,0:T(8,128)(2,1)S(1)} %get-tuple-element.55), channel_id=1, source_target_pairs={{0,96},{1,25},{2,98},{3,27},{4,100},{5,29},{6,102},{7,31},{8,104},... | collective-permute-start | bytes 1572872 | tf_op jit(solution)/shard_map/ppermute | solution.py:187
  93.9 13.8 %collective-permute-start.6 = (bf16[8,32,1024]{2,1,0:T(8,128)(2,1)S(1)}, bf16[8,32,1024]{2,1,0:T(8,128)(2,1)S(1)}, u32[]{:S(2)}, u32[]{:S(2)}) collective-permute-start(bf16[8,32,1024]{2,1,0:T(8,128)(2,1)S(1)} %get-tuple-element.51), channel_id=1, source_target_pairs={{0,32},{1,9},{2,34},{3,11},{4,36},{5,13},{6,38},{7,15},{8,40},{9,1... | collective-permute-start | bytes 1572872 | tf_op jit(solution)/shard_map/ppermute | solution.py:187
  109.0 0.8 copy-start.5
  109.9 12.0 %collective-permute-start.10 = (bf16[8,32,1024]{2,1,0:T(8,128)(2,1)}, bf16[8,32,1024]{2,1,0:T(8,128)(2,1)}, u32[]{:S(2)}, u32[]{:S(2)}) collective-permute-start(bf16[8,32,1024]{2,1,0:T(8,128)(2,1)} %get-tuple-element.63), channel_id=1, source_target_pairs={{0,16},{1,65},{2,18},{3,67},{4,20},{5,69},{6,22},{7,71},{8,24},{9,... | collective-permute-start | bytes 1572872 | tf_op jit(solution)/shard_map/ppermute | solution.py:187
  110.2 28.2 %collective-permute-start.11 = (bf16[8,32,1024]{2,1,0:T(8,128)(2,1)}, bf16[8,32,1024]{2,1,0:T(8,128)(2,1)}, u32[]{:S(2)}, u32[]{:S(2)}) collective-permute-start(bf16[8,32,1024]{2,1,0:T(8,128)(2,1)} %get-tuple-element.64), channel_id=1, source_target_pairs={{0,24},{1,97},{2,26},{3,99},{4,28},{5,101},{6,30},{7,103},{8,0},{9... | collective-permute-start | bytes 1572872 | tf_op jit(solution)/shard_map/ppermute | solution.py:187
  112.6 27.5 %collective-permute-start.9 = (bf16[8,32,1024]{2,1,0:T(8,128)(2,1)}, bf16[8,32,1024]{2,1,0:T(8,128)(2,1)}, u32[]{:S(2)}, u32[]{:S(2)}) collective-permute-start(bf16[8,32,1024]{2,1,0:T(8,128)(2,1)} %get-tuple-element.56), channel_id=1, source_target_pairs={{0,8},{1,33},{2,10},{3,35},{4,12},{5,37},{6,14},{7,39},{8,16},{9,4... | collective-permute-start | bytes 1572872 | tf_op jit(solution)/shard_map/ppermute | solution.py:187
  115.8 32.3 %collective-permute-start.13 = (bf16[8,48,1024]{2,1,0:T(8,128)(2,1)}, bf16[8,48,1024]{2,1,0:T(8,128)(2,1)S(1)}, u32[]{:S(2)}, u32[]{:S(2)}) collective-permute-start(bf16[8,48,1024]{2,1,0:T(8,128)(2,1)} %get-tuple-element.67), channel_id=1, source_target_pairs={{0,64},{1,17},{2,66},{3,19},{4,68},{5,21},{6,70},{7,23},{8,72},{9,... | collective-permute-start | bytes 2359304 | tf_op jit(solution)/shard_map/ppermute | solution.py:187
  116.5 32.6 %collective-permute-start.14 = (bf16[8,48,1024]{2,1,0:T(8,128)(2,1)}, bf16[8,48,1024]{2,1,0:T(8,128)(2,1)}, u32[]{:S(2)}, u32[]{:S(2)}) collective-permute-start(bf16[8,48,1024]{2,1,0:T(8,128)(2,1)} %get-tuple-element.68), channel_id=1, source_target_pairs={{0,96},{1,25},{2,98},{3,27},{4,100},{5,29},{6,102},{7,31},{8,104},... | collective-permute-start | bytes 2359304 | tf_op jit(solution)/shard_map/ppermute | solution.py:187
  121.8 18.2 %copy-start.1 = (bf16[16,128,1024]{2,1,0:T(8,128)(2,1)S(1)}, bf16[16,128,1024]{2,1,0:T(8,128)(2,1)}, u32[]{:S(2)}) copy-start(bf16[16,128,1024]{2,1,0:T(8,128)(2,1)} %other_ref.5) | copy-start | bytes 12582916
  121.8 18.2 %copy-start.6 = (bf16[8,32,1024]{2,1,0:T(8,128)(2,1)S(1)}, bf16[8,32,1024]{2,1,0:T(8,128)(2,1)}, u32[]{:S(2)}) copy-start(bf16[8,32,1024]{2,1,0:T(8,128)(2,1)} %copy-done.5) | copy-start | bytes 1572868
  121.9 18.2 %copy-start.8 = (s32[32]{0:T(128)S(1)}, s32[32]{0:T(128)}, u32[]{:S(2)}) copy-start(s32[32]{0:T(128)} %find.1.ids_ref) | copy-start | bytes 388
  121.9 27.2 %collective-permute-start.12 = (bf16[8,48,1024]{2,1,0:T(8,128)(2,1)}, bf16[8,48,1024]{2,1,0:T(8,128)(2,1)}, u32[]{:S(2)}, u32[]{:S(2)}) collective-permute-start(bf16[8,48,1024]{2,1,0:T(8,128)(2,1)} %get-tuple-element.59), channel_id=1, source_target_pairs={{0,32},{1,9},{2,34},{3,11},{4,36},{5,13},{6,38},{7,15},{8,40},{9,1... | collective-permute-start | bytes 2359304 | tf_op jit(solution)/shard_map/ppermute | solution.py:187
  143.2 26.6 %all-to-all-start.3 = ((bf16[8,2,48,1024]{3,2,1,0:T(8,128)(2,1)}), bf16[8,2,48,1024]{3,2,1,0:T(8,128)(2,1)S(1)}, u32[]{:S(2)}, u32[]{:S(2)}) async-start(bf16[8,2,48,1024]{3,2,1,0:T(8,128)(2,1)} %sweeps.3), calls=%async_computation.3 | async-start | bytes 3145728 | tf_op jit(solution)/shard_map/all_to_all | solution.py:250
  148.2 0.9 copy-start.3
  149.1 1.1 copy-start.4
  153.1 20.3 %collective-permute-start.19 = (bf16[8,48,1024]{2,1,0:T(8,128)(2,1)}, bf16[8,48,1024]{2,1,0:T(8,128)(2,1)S(1)}, u32[]{:S(2)}, u32[]{:S(2)}) collective-permute-start(bf16[8,48,1024]{2,1,0:T(8,128)(2,1)} %get-tuple-element.86), channel_id=1, source_target_pairs={{0,16},{1,65},{2,18},{3,67},{4,20},{5,69},{6,22},{7,71},{8,24},{9,... | collective-permute-start | bytes 2359304 | tf_op jit(solution)/shard_map/ppermute | solution.py:187
  153.1 21.3 %collective-permute-start.20 = (bf16[8,48,1024]{2,1,0:T(8,128)(2,1)}, bf16[8,48,1024]{2,1,0:T(8,128)(2,1)}, u32[]{:S(2)}, u32[]{:S(2)}) collective-permute-start(bf16[8,48,1024]{2,1,0:T(8,128)(2,1)} %get-tuple-element.87), channel_id=1, source_target_pairs={{0,24},{1,97},{2,26},{3,99},{4,28},{5,101},{6,30},{7,103},{8,0},{9... | collective-permute-start | bytes 2359304 | tf_op jit(solution)/shard_map/ppermute | solution.py:187
  155.8 20.8 %collective-permute-start.18 = (bf16[8,48,1024]{2,1,0:T(8,128)(2,1)}, bf16[8,48,1024]{2,1,0:T(8,128)(2,1)}, u32[]{:S(2)}, u32[]{:S(2)}) collective-permute-start(bf16[8,48,1024]{2,1,0:T(8,128)(2,1)} %get-tuple-element.73), channel_id=1, source_target_pairs={{0,8},{1,33},{2,10},{3,35},{4,12},{5,37},{6,14},{7,39},{8,16},{9,4... | collective-permute-start | bytes 2359304 | tf_op jit(solution)/shard_map/ppermute | solution.py:187
  169.8 6.9 %copy-start.2 = (bf16[16,128,1024]{2,1,0:T(8,128)(2,1)S(1)}, bf16[16,128,1024]{2,1,0:T(8,128)(2,1)}, u32[]{:S(2)}) copy-start(bf16[16,128,1024]{2,1,0:T(8,128)(2,1)} %other_ref.5) | copy-start | bytes 12582916
  171.5 20.5 %collective-permute-start.15 = (bf16[8,48,1024]{2,1,0:T(8,128)(2,1)S(1)}, bf16[8,48,1024]{2,1,0:T(8,128)(2,1)S(1)}, u32[]{:S(2)}, u32[]{:S(2)}) collective-permute-start(bf16[8,48,1024]{2,1,0:T(8,128)(2,1)S(1)} %get-tuple-element.78), channel_id=1, source_target_pairs={{0,32},{1,9},{2,34},{3,11},{4,36},{5,13},{6,38},{7,15},{8,40},{9,1... | collective-permute-start | bytes 2359304 | tf_op jit(solution)/shard_map/ppermute | solution.py:187
  172.3 19.6 %collective-permute-start.16 = (bf16[8,48,1024]{2,1,0:T(8,128)(2,1)S(1)}, bf16[8,48,1024]{2,1,0:T(8,128)(2,1)S(1)}, u32[]{:S(2)}, u32[]{:S(2)}) collective-permute-start(bf16[8,48,1024]{2,1,0:T(8,128)(2,1)S(1)} %get-tuple-element.79), channel_id=1, source_target_pairs={{0,64},{1,17},{2,66},{3,19},{4,68},{5,21},{6,70},{7,23},{8,72},{9,... | collective-permute-start | bytes 2359304 | tf_op jit(solution)/shard_map/ppermute | solution.py:187
  173.4 20.7 %collective-permute-start.17 = (bf16[8,48,1024]{2,1,0:T(8,128)(2,1)S(1)}, bf16[8,48,1024]{2,1,0:T(8,128)(2,1)S(1)}, u32[]{:S(2)}, u32[]{:S(2)}) collective-permute-start(bf16[8,48,1024]{2,1,0:T(8,128)(2,1)S(1)} %get-tuple-element.80), channel_id=1, source_target_pairs={{0,96},{1,25},{2,98},{3,27},{4,100},{5,29},{6,102},{7,31},{8,104},... | collective-permute-start | bytes 2359304 | tf_op jit(solution)/shard_map/ppermute | solution.py:187
  194.3 20.5 %collective-permute-start.21 = (bf16[8,48,1024]{2,1,0:T(8,128)(2,1)S(1)}, bf16[8,48,1024]{2,1,0:T(8,128)(2,1)S(1)}, u32[]{:S(2)}, u32[]{:S(2)}) collective-permute-start(bf16[8,48,1024]{2,1,0:T(8,128)(2,1)S(1)} %get-tuple-element.89), channel_id=1, source_target_pairs={{0,8},{1,33},{2,10},{3,35},{4,12},{5,37},{6,14},{7,39},{8,16},{9,4... | collective-permute-start | bytes 2359304 | tf_op jit(solution)/shard_map/ppermute | solution.py:187
  195.6 19.1 %collective-permute-start.22 = (bf16[8,48,1024]{2,1,0:T(8,128)(2,1)S(1)}, bf16[8,48,1024]{2,1,0:T(8,128)(2,1)S(1)}, u32[]{:S(2)}, u32[]{:S(2)}) collective-permute-start(bf16[8,48,1024]{2,1,0:T(8,128)(2,1)S(1)} %get-tuple-element.90), channel_id=1, source_target_pairs={{0,16},{1,65},{2,18},{3,67},{4,20},{5,69},{6,22},{7,71},{8,24},{9,... | collective-permute-start | bytes 2359304 | tf_op jit(solution)/shard_map/ppermute | solution.py:187
  196.3 20.6 %collective-permute-start.23 = (bf16[8,48,1024]{2,1,0:T(8,128)(2,1)S(1)}, bf16[8,48,1024]{2,1,0:T(8,128)(2,1)S(1)}, u32[]{:S(2)}, u32[]{:S(2)}) collective-permute-start(bf16[8,48,1024]{2,1,0:T(8,128)(2,1)S(1)} %get-tuple-element.91), channel_id=1, source_target_pairs={{0,24},{1,97},{2,26},{3,99},{4,28},{5,101},{6,30},{7,103},{8,0},{9... | collective-permute-start | bytes 2359304 | tf_op jit(solution)/shard_map/ppermute | solution.py:187

commit v3 on v2

--- a/solution.py
+++ b/solution.py
@@ -10,11 +10,14 @@
 CAP = 2
 ITERS = 6
 SIDE = 4
+SWEEP_MIB = 24
+PACK_MIB = 12
+GROUP_MIB = 12
 CHUNKS = (32, 48, 48)
-AHEAD = 2
 VMEM = pl.BlockSpec(memory_space=pltpu.VMEM)
 SMEM = pl.BlockSpec(memory_space=pltpu.SMEM)
-ANY = pl.BlockSpec(memory_space=pl.ANY)
+HBM = pl.BlockSpec(memory_space=pltpu.HBM)
+TOKEN = jax.ShapeDtypeStruct((8, 128), jnp.float32)
 
 
 def params(mib):
@@ -25,35 +28,55 @@
     return pl.CostEstimate(flops=int(flops), bytes_accessed=int(nbytes), transcendentals=0)
 
 
-def sweep_kernel(first, rows, vertex_ref, bubble_ref, ladder_ref):
+def sweep_kernel(first, rows, vertex_ref, bubble_ref, *rest):
+    ladder_ref, matrices, results, sems = rest[-4:]
     blocks, count, freq, width = vertex_ref.shape
-    order = blocks * freq
+    reads = [
+        pltpu.make_async_copy(vertex_ref.at[:, index], matrices.at[index], sems.at[0, index])
+        for index in range(count)
+    ]
+    writes = [
+        pltpu.make_async_copy(results.at[index], ladder_ref.at[:, index], sems.at[1, index])
+        for index in range(count)
+    ]
+    for read in reads:
+        read.start()
     for index in range(count):
+        reads[index].wait()
         scales = bubble_ref[index : index + 1, :]
-        start = vertex_ref[:, index, first : first + rows].reshape(blocks * rows, width).astype(jnp.float32)
+        start = matrices[index, :, first : first + rows].reshape(blocks * rows, width).astype(jnp.float32)
         current = start
         for _ in range(ITERS):
             scaled = (current * scales).astype(jnp.bfloat16)
-            matrix = vertex_ref[:, index].reshape(order, width)
+            matrix = matrices[index].reshape(blocks * freq, width)
             current = start + jnp.dot(scaled, matrix, preferred_element_type=jnp.float32)
-        ladder_ref[:, index] = current.astype(jnp.bfloat16).reshape(blocks, rows, width)
-
-
-def sweeps(vertex, bubble, first, rows):
+        results[index] = current.astype(jnp.bfloat16).reshape(blocks, rows, width)
+        writes[index].start()
+    for write in writes:
+        write.wait()
+
+
+def sweeps(vertex, bubble, first, rows, earlier=()):
     blocks, count, freq, width = vertex.shape
     return pl.pallas_call(
         functools.partial(sweep_kernel, first, rows),
-        in_specs=[VMEM, VMEM],
-        out_specs=VMEM,
+        in_specs=[HBM, VMEM] + [HBM] * len(earlier),
+        out_specs=HBM,
         out_shape=jax.ShapeDtypeStruct((blocks, count, rows, width), jnp.bfloat16),
-        compiler_params=params(32),
+        scratch_shapes=[
+            pltpu.VMEM((count, blocks, freq, width), jnp.bfloat16),
+            pltpu.VMEM((count, blocks, rows, width), jnp.bfloat16),
+            pltpu.SemaphoreType.DMA((2, count)),
+        ],
+        compiler_params=params(SWEEP_MIB),
         cost_estimate=cost(2 * ITERS * count * blocks * rows * width * width, 2 * vertex.size),
         name="sweeps",
-    )(vertex, bubble)
+    )(vertex, bubble, *earlier)
 
 
 def pack_kernel(first, rows, place_ref, crossing_ref, part_ref, *rest):
-    ladder_ref, outs, used, sem = rest[-SIDE - 3], rest[-SIDE - 2 : -2], rest[-2], rest[-1]
+    ladder_ref, outs, token, used, sem = rest[-SIDE - 4], rest[-SIDE - 3 : -3], rest[-3], rest[-2], rest[-1]
+    token[...] = jnp.zeros_like(token)
     q_local = part_ref.shape[0]
     keep = pltpu.make_async_copy(part_ref, ladder_ref.at[:, first : first + rows], sem)
     keep.start()
@@ -79,7 +102,7 @@
     keep.wait()
 
 
-def pack(place, crossing, part, ladder, first, freq):
+def pack(place, crossing, part, ladder, first, freq, earlier=()):
     q_local, rows, width = part.shape
     slots = SIDE * SIDE * CAP
     whole = jax.ShapeDtypeStruct((q_local, freq, width), jnp.bfloat16)
@@ -87,16 +110,16 @@
     carried = [] if ladder is None else [ladder]
     results = pl.pallas_call(
         functools.partial(pack_kernel, first, rows),
-        in_specs=[SMEM, SMEM, VMEM] + [ANY] * len(carried),
-        out_specs=[ANY] + [VMEM] * SIDE,
-        out_shape=[whole] + [piece] * SIDE,
+        in_specs=[SMEM, SMEM, VMEM] + [HBM] * (len(carried) + len(earlier)),
+        out_specs=[HBM] + [VMEM] * (SIDE + 1),
+        out_shape=[whole] + [piece] * SIDE + [TOKEN],
         scratch_shapes=[pltpu.SMEM((slots,), jnp.int32), pltpu.SemaphoreType.DMA],
         input_output_aliases={3: 0} if carried else {},
-        compiler_params=params(32),
+        compiler_params=params(PACK_MIB),
         cost_estimate=cost(0, 8 * part.size),
         name="pack",
-    )(place, crossing, part, *carried)
-    return results[0], list(results[1:])
+    )(place, crossing, part, *carried, *earlier)
+    return results[0], list(results[1:-1]), results[-1]
 
 
 def collect_kernel(first, rows, ids_ref, other_ref, *rest):
@@ -120,25 +143,24 @@
     write.wait()
 
 
-def collect(ids, other, pieces, crossed, first):
+def collect(ids, other, pieces, crossed, first, earlier=()):
     q_local, freq, width = other.shape
     rows = pieces[0].shape[1]
-    carried = [] if crossed is None else [crossed]
     return pl.pallas_call(
         functools.partial(collect_kernel, first, rows),
-        in_specs=[SMEM, ANY] + [VMEM] * SIDE + [ANY] * len(carried),
-        out_specs=ANY,
+        in_specs=[SMEM, HBM] + [VMEM] * SIDE + [HBM] * (len(crossed) + len(earlier)),
+        out_specs=HBM,
         out_shape=jax.ShapeDtypeStruct(other.shape, jnp.bfloat16),
         scratch_shapes=[
             pltpu.VMEM((q_local, rows, width), jnp.float32),
             pltpu.VMEM((q_local, rows, width), jnp.bfloat16),
             pltpu.SemaphoreType.DMA((2,)),
         ],
-        input_output_aliases={2 + SIDE: 0} if carried else {},
-        compiler_params=params(40),
+        input_output_aliases={2 + SIDE: 0} if crossed else {},
+        compiler_params=params(16),
         cost_estimate=cost(0, 16 * q_local * rows * width),
         name="collect",
-    )(ids, other, *pieces, *carried)
+    )(ids, other, *pieces, *crossed, *earlier)
 
 
 def find_kernel(place_ref, everyone_ref, ids_ref, seen):
@@ -188,22 +210,24 @@
 
 
 def regroup_kernel(*refs):
+    pieces, outs, token = refs[:SIDE], refs[-SIDE - 1 : -1], refs[-1]
+    token[...] = jnp.zeros_like(token)
     for two in range(SIDE):
         for one in range(SIDE):
-            refs[SIDE + two][one * CAP : one * CAP + CAP] = refs[one][two * CAP : two * CAP + CAP]
-
-
-def regroup(pieces):
+            outs[two][one * CAP : one * CAP + CAP] = pieces[one][two * CAP : two * CAP + CAP]
+
+
+def regroup(pieces, earlier=()):
     shape = jax.ShapeDtypeStruct(pieces[0].shape, pieces[0].dtype)
     return pl.pallas_call(
         regroup_kernel,
-        in_specs=[VMEM] * SIDE,
-        out_specs=[VMEM] * SIDE,
-        out_shape=[shape] * SIDE,
-        compiler_params=params(32),
+        in_specs=[VMEM] * SIDE + [HBM] * len(earlier),
+        out_specs=[VMEM] * (SIDE + 1),
+        out_shape=[shape] * SIDE + [TOKEN],
+        compiler_params=params(GROUP_MIB),
         cost_estimate=cost(0, 4 * SIDE * pieces[0].size),
         name="regroup",
-    )(*pieces)
+    )(*pieces, *earlier)
 
 
 def after(value, *earlier):
@@ -213,13 +237,6 @@
 def spread(pieces, phase):
     moved = {step: shift(pieces[step], step, phase) for step in (1, 3, 2)}
     return [pieces[0]] + [moved[step] for step in range(1, SIDE)]
-
-
-def exchange(pieces, earlier=()):
-    again = regroup(spread(pieces, 0))
-    if earlier:
-        again, _ = lax.optimization_barrier((again, earlier))
-    return spread(again, 1), again[1]
 
 
 def local(vertex, bubble, vertex_cross, crossing):
@@ -237,28 +254,29 @@
     )
     scales = lax.dynamic_slice_in_dim(bubble, lax.axis_index("row") * mine, mine, 0)
     whole, scales, ids = lax.optimization_barrier((whole, scales, ids))
-    ladder = None
-    packed, summed, halfway = [], [], ()
     firsts = [sum(CHUNKS[:step]) for step in range(len(CHUNKS))]
-    ready = {step: sweeps(whole, scales, firsts[step], rows) for step, rows in enumerate(CHUNKS)}
-    for step, rows in enumerate(CHUNKS):
-        first, solved = firsts[step], ready[step]
-        if step >= 1:
-            solved = after(solved, packed[step - 1])
-        if step >= 2:
-            solved, summed[step - 2] = lax.optimization_barrier((solved, summed[step - 2]))
+    chunks = list(zip(firsts, CHUNKS))
+
+    def back(solved, rows):
         part = lax.all_to_all(solved, "row", split_axis=0, concat_axis=0, tiled=True)
-        part = part.reshape(q_local, rows, width)
-        part = after(part, *halfway)
-        if step == 0:
-            for other in range(1, min(AHEAD, len(CHUNKS))):
-                part, ready[other] = lax.optimization_barrier((part, ready[other]))
-        ladder, outgoing = pack(place, crossing, part, ladder, first, freq)
-        packed.append(outgoing[1])
-        pieces, half = exchange(outgoing, summed[step - 1 : step])
-        halfway = (half,)
-        summed.append(collect(ids, vertex_cross, pieces, summed[-1] if summed else None, first))
-    return ladder, summed[-1]
+        return part.reshape(q_local, rows, width)
+
+    solved = [sweeps(whole, scales, *chunk) for chunk in chunks[:2]]
+    ladder, crossed, arrived, halfway = None, [], [], []
+    for step, (first, rows) in enumerate(chunks):
+        part = back(solved[step], rows)
+        ladder, outgoing, token = pack(
+            place, crossing, part, ladder, first, freq, (solved[1:] if step == 0 else []) + halfway
+        )
+        ahead = [sweeps(whole, scales, *chunk, [token]) for chunk in chunks[step + 2 : step + 3]]
+        solved += ahead
+        moved = spread(outgoing, 0)
+        *again, token = regroup(moved, ahead + arrived[1:])
+        halfway = [token]
+        if arrived:
+            crossed = [collect(ids, vertex_cross, arrived, crossed, firsts[step - 1], halfway)]
+        arrived = spread(again, 1)
+    return ladder, collect(ids, vertex_cross, arrived, crossed, firsts[-1])
 
 
 def solution(mesh):

time: 221 us -> 220 us (level)
  waiting for transfers between devices: 111 us -> 102 us
  starting transfers between devices: 41 us -> 49.8 us
  Pallas kernels: 61.9 us -> 59.2 us
    all_to_all x3, waiting for transfers between devices: 16.4 us -> 3.07 us  [back(): lax.all_to_all(solved, 'row', split_axis=0, concat_axis=0, tiled=True)]
    ppermute x24, starting transfers between devices: 23.3 us -> 32.3 us  [shift(): return lax.ppermute(value, ('boson', 'row'), pairs)]
    ppermute x24, waiting for transfers between devices: 63.6 us -> 68 us  [shift(): return lax.ppermute(value, ('boson', 'row'), pairs)]
  transfers between devices with their start and end apart: 28 -> 28, of which waited for: 20 -> 18; matrix products, arithmetic and copies ran while one was open for 1% -> 1% of each run, Pallas kernels for 22% -> 22%
where the time goes in v3:
time: 220 us; the launch traced here: 217 us
  waiting for transfers between devices  102 us (46%)
  Pallas kernels  59.2 us (27%)
  starting transfers between devices  49.8 us (23%)
  local copies, waits for them, and re-layouts  3.38 us (2%)
    ppermute x24, waiting for transfers between devices, shift(): return lax.ppermute(value, ('boson', 'row'), pairs)  68 us
    pallas_call x3, Pallas kernels, sweeps(): pl.pallas_call(functools.partial(sweep_kernel, first, rows), in_specs=[HB...  34.6 us
    ppermute x24, starting transfers between devices, shift(): return lax.ppermute(value, ('boson', 'row'), pairs)  32.3 us
    all_to_all x1, waiting for transfers between devices, local(): lax.all_to_all(vertex.reshape(n_row, mine, freq, width), 'row', split_axi...  30.9 us
    all_to_all x3, starting transfers between devices, back(): lax.all_to_all(solved, 'row', split_axis=0, concat_axis=0, tiled=True)  12 us
    pallas_call x3, Pallas kernels, collect(): pl.pallas_call(functools.partial(collect_kernel, first, rows), in_specs=[...  8.36 us
    pallas_call x3, Pallas kernels, pack(): pl.pallas_call(functools.partial(pack_kernel, first, rows), in_specs=[SME...  6.96 us
    all_to_all x1, starting transfers between devices, local(): lax.all_to_all(vertex.reshape(n_row, mine, freq, width), 'row', split_axi...  5.46 us
  transfers between devices with their start and end apart: 28, of which 18 were waited for; matrix products, arithmetic and copies ran while one was open for 1% of the time, Pallas kernels for 22%

profile of v3, /device:TPU:20, one launch (start us, length us, event | category | flops | bytes accessed | tf_op | source)
XLA Modules:
  0.0 216.8 jit_solution(12843439136104651125)
XLA Ops:
  0.7 5.5 %all-to-all-start = ((bf16[8,2,128,1024]{3,2,1,0:T(8,128)(2,1)}), bf16[8,2,128,1024]{3,2,1,0:T(8,128)(2,1)}, u32[]{:S(2)}, u32[]{:S(2)}) async-start(bf16[8,2,128,1024]{3,2,1,0:T(8,128)(2,1)} %bitcast.28), calls=%async_computation | async-start | bytes 8388608 | tf_op jit(solution)/shard_map/all_to_all | solution.py:252
  6.7 2.7 %collective-permute-start.1 = (s32[16]{0:T(128)S(1)}, s32[16]{0:T(128)S(1)}, u32[]{:S(2)}, u32[]{:S(2)}) collective-permute-start(s32[16]{0:T(128)S(1)} %bitcast.22), channel_id=1, source_target_pairs={{0,64},{1,17},{2,66},{3,19},{4,68},{5,21},{6,70},{7,23},{8,72},{9,... | collective-permute-start | bytes 200 | tf_op jit(solution)/shard_map/ppermute | solution.py:209
  9.7 2.0 collective-permute-done.1
  11.8 1.2 collective-permute-done
  13.4 2.2 %collective-permute-start.3 = (s32[4,16]{1,0:T(4,128)S(1)}, s32[4,16]{1,0:T(4,128)S(1)}, u32[]{:S(2)}, u32[]{:S(2)}) collective-permute-start(s32[4,16]{1,0:T(4,128)S(1)} %get-tuple-element.71), channel_id=1, source_target_pairs={{0,8},{1,33},{2,10},{3,35},{4,12},{5,37},{6,14},{7,39},{8,16},{9,4... | collective-permute-start | bytes 776 | tf_op jit(solution)/shard_map/ppermute | solution.py:209
  16.5 1.7 collective-permute-done.4
  18.2 1.2 collective-permute-done.5
  20.0 5.0 %find.1.ids_ref = s32[32]{0:T(128)} custom-call(s32[4]{0:T(128)} %pad_add_fusion.2.place_ref, s32[4,4,16]{2,1,0:T(4,128)} %pad_add_fusion.everyone_ref), custom_call_target="tpu_custom_call" | custom-call | tf_op jit(solution)/shard_map/find/pallas_call | solution.py:188
  25.0 30.9 %all-to-all-done.vertex_ref = bf16[8,2,128,1024]{3,2,1,0:T(8,128)(2,1)} async-done(((bf16[8,2,128,1024]{3,2,1,0:T(8,128)(2,1)}), bf16[8,2,128,1024]{3,2,1,0:T(8,128)(2,1)}, u32[]{:S(2)}, u32[]{:S(2)}) %all-to-all-start) | async-done | bytes 4194336 | tf_op jit(solution)/shard_map/all_to_all | solution.py:252
  55.9 9.3 %sweeps.3 = bf16[8,2,32,1024]{3,2,1,0:T(8,128)(2,1)} custom-call(bf16[8,2,128,1024]{3,2,1,0:T(8,128)(2,1)} %all-to-all-done.vertex_ref, f32[2,1024]{1,0:T(2,128)S(1)} %constant_dynamic-slice_fusion.bubble_ref), custom_call_target="tpu_custom_call" | custom-call | flops 6442450944 | bytes 4194304 | tf_op jit(solution)/shard_map/sweeps/pallas_call | solution.py:61
  65.2 3.8 %all-to-all-start.1 = ((bf16[8,2,32,1024]{3,2,1,0:T(8,128)(2,1)}), bf16[8,2,32,1024]{3,2,1,0:T(8,128)(2,1)S(1)}, u32[]{:S(2)}, u32[]{:S(2)}) async-start(bf16[8,2,32,1024]{3,2,1,0:T(8,128)(2,1)} %sweeps.3), calls=%async_computation.1 | async-start | bytes 2097152 | tf_op jit(solution)/shard_map/all_to_all | solution.py:261
  69.0 12.6 %sweeps.4.rest_0_ = bf16[8,2,48,1024]{3,2,1,0:T(8,128)(2,1)} custom-call(bf16[8,2,128,1024]{3,2,1,0:T(8,128)(2,1)} %all-to-all-done.vertex_ref, f32[2,1024]{1,0:T(2,128)S(1)} %constant_dynamic-slice_fusion.bubble_ref), custom_call_target="tpu_custom_call" | custom-call | flops 9663676416 | bytes 4194304 | tf_op jit(solution)/shard_map/sweeps/pallas_call | solution.py:61
  81.6 3.1 %all-to-all-done.1 = bf16[8,2,32,1024]{3,2,1,0:T(8,128)(2,1)S(1)} async-done(((bf16[8,2,32,1024]{3,2,1,0:T(8,128)(2,1)}), bf16[8,2,32,1024]{3,2,1,0:T(8,128)(2,1)S(1)}, u32[]{:S(2)}, u32[]{:S(2)}) %all-to-all-start.1) | async-done | bytes 1048608 | tf_op jit(solution)/shard_map/all_to_all | solution.py:261
  84.7 3.6 %all-to-all-start.3 = ((bf16[8,2,48,1024]{3,2,1,0:T(8,128)(2,1)}), bf16[8,2,48,1024]{3,2,1,0:T(8,128)(2,1)S(1)}, u32[]{:S(2)}, u32[]{:S(2)}) async-start(bf16[8,2,48,1024]{3,2,1,0:T(8,128)(2,1)} %sweeps.4.rest_0_), calls=%async_computation.3 | async-start | bytes 3145728 | tf_op jit(solution)/shard_map/all_to_all | solution.py:261
  88.3 1.5 pack.3
  89.8 1.3 collective-permute-start.6
  91.8 1.1 collective-permute-start.8
  93.0 12.7 %sweeps.5.refs_4_ = bf16[8,2,48,1024]{3,2,1,0:T(8,128)(2,1)} custom-call(bf16[8,2,128,1024]{3,2,1,0:T(8,128)(2,1)} %all-to-all-done.vertex_ref, f32[2,1024]{1,0:T(2,128)S(1)} %constant_dynamic-slice_fusion.bubble_ref, f32[8,128]{1,0:T(8,128)S(1)} %get-tuple-element.38.rest_0_), custom_call_target="tpu_custom_call" | custom-call | flops 9663676416 | bytes 4194304 | tf_op jit(solution)/shard_map/sweeps/pallas_call | solution.py:61
  105.7 1.1 collective-permute-done.8.refs_3_
  106.8 0.9 regroup.3
  110.1 1.3 collective-permute-start.12
  111.4 3.1 %pack.4 = (bf16[16,128,1024]{2,1,0:T(8,128)(2,1)}, bf16[8,48,1024]{2,1,0:T(8,128)(2,1)S(1)}, bf16[8,48,1024]{2,1,0:T(8,128)(2,1)}, bf16[8,48,1024]{2,1,0:T(8,128...) custom-call(s32[4]{0:T(128)S(1)} %copy-done.12, s32[16]{0:T(128)S(1)} %bitcast.26, ...), custom_call_target="tpu_custom_call", output_to_operand_aliasing={{0}: (3, {})} | custom-call | bytes 6291456 | tf_op jit(solution)/shard_map/pack/pallas_call | solution.py:111
  114.6 1.1 collective-permute-start.9
  115.7 1.5 collective-permute-start.10
  117.2 2.1 collective-permute-start.11
  119.2 4.7 %all-to-all-start.2 = ((bf16[8,2,48,1024]{3,2,1,0:T(8,128)(2,1)}), bf16[8,2,48,1024]{3,2,1,0:T(8,128)(2,1)S(1)}, u32[]{:S(2)}, u32[]{:S(2)}) async-start(bf16[8,2,48,1024]{3,2,1,0:T(8,128)(2,1)} %sweeps.5.refs_4_), calls=%async_computation.2 | async-start | bytes 3145728 | tf_op jit(solution)/shard_map/all_to_all | solution.py:261
  124.6 1.0 collective-permute-start.14
  125.6 15.0 %collective-permute-done.13.refs_5_.rest_2_ = bf16[8,32,1024]{2,1,0:T(8,128)(2,1)S(1)} collective-permute-done((bf16[8,32,1024]{2,1,0:T(8,128)(2,1)}, bf16[8,32,1024]{2,1,0:T(8,128)(2,1)S(1)}, u32[]{:S(2)}, u32[]{:S(2)}) %collective-permute-start.13) | collective-permute-done | bytes 524320 | tf_op jit(solution)/shard_map/ppermute | solution.py:209
  140.6 5.7 %collective-permute-done.14.refs_6_.rest_3_ = bf16[8,32,1024]{2,1,0:T(8,128)(2,1)S(1)} collective-permute-done((bf16[8,32,1024]{2,1,0:T(8,128)(2,1)}, bf16[8,32,1024]{2,1,0:T(8,128)(2,1)S(1)}, u32[]{:S(2)}, u32[]{:S(2)}) %collective-permute-start.14) | collective-permute-done | bytes 524320 | tf_op jit(solution)/shard_map/ppermute | solution.py:209
  146.2 1.4 collective-permute-done.11.refs_3_
  147.6 3.1 %regroup.4 = (bf16[8,48,1024]{2,1,0:T(8,128)(2,1)S(1)}, bf16[8,48,1024]{2,1,0:T(8,128)(2,1)}, bf16[8,48,1024]{2,1,0:T(8,128)(2,1)}, bf16[8,48,1024]{2,1,0:T(8,128)(2,1)}, f32[8,128]{1,0:T(8,128)S(1)}) custom-call(bf16[8,48,1024]{2,1,0:T(8,128)(2,1)S(1)} %get-tuple-element.46.refs_0_, bf16[8,48,1024]{2,1,0:T(8,128)(2,1)} %collective-permute-done.9.refs_1_, ...), custom_call_target="tpu_custom_call" | custom-call | bytes 6291456 | tf_op jit(solution)/shard_map/regroup/pallas_call | solution.py:222
  150.8 0.9 copy-done.8
  151.9 2.0 collective-permute-start.19
  153.9 1.5 collective-permute-start.20
  155.4 2.3 %pack.5 = (bf16[16,128,1024]{2,1,0:T(8,128)(2,1)}, bf16[8,48,1024]{2,1,0:T(8,128)(2,1)S(1)}, bf16[8,48,1024]{2,1,0:T(8,128)(2,1)S(1)}, bf16[8,48,1024]{2,1,0:T(8...) custom-call(s32[4]{0:T(128)S(1)} %copy-done.12, ...), custom_call_target="tpu_custom_call", output_to_operand_aliasing={{0}: (3, {})} | custom-call | bytes 6291456 | tf_op jit(solution)/shard_map/pack/pallas_call | solution.py:111
  157.7 3.3 %collective-permute-start.15 = (bf16[8,48,1024]{2,1,0:T(8,128)(2,1)S(1)}, bf16[8,48,1024]{2,1,0:T(8,128)(2,1)S(1)}, u32[]{:S(2)}, u32[]{:S(2)}) collective-permute-start(bf16[8,48,1024]{2,1,0:T(8,128)(2,1)S(1)} %get-tuple-element.57), channel_id=1, source_target_pairs={{0,32},{1,9},{2,34},{3,11},{4,36},{5,13},{6,38},{7,15},{8,40},{9,1... | collective-permute-start | bytes 2359304 | tf_op jit(solution)/shard_map/ppermute | solution.py:209
  161.3 4.6 %collective-permute-done.18.refs_4_.rest_1_ = bf16[8,48,1024]{2,1,0:T(8,128)(2,1)S(1)} collective-permute-done((bf16[8,48,1024]{2,1,0:T(8,128)(2,1)}, bf16[8,48,1024]{2,1,0:T(8,128)(2,1)S(1)}, u32[]{:S(2)}, u32[]{:S(2)}) %collective-permute-start.18) | collective-permute-done | bytes 786464 | tf_op jit(solution)/shard_map/ppermute | solution.py:209
  166.0 4.6 %collective-permute-start.17 = (bf16[8,48,1024]{2,1,0:T(8,128)(2,1)S(1)}, bf16[8,48,1024]{2,1,0:T(8,128)(2,1)S(1)}, u32[]{:S(2)}, u32[]{:S(2)}) collective-permute-start(bf16[8,48,1024]{2,1,0:T(8,128)(2,1)S(1)} %get-tuple-element.59), channel_id=1, source_target_pairs={{0,96},{1,25},{2,98},{3,27},{4,100},{5,29},{6,102},{7,31},{8,104},... | collective-permute-start | bytes 2359304 | tf_op jit(solution)/shard_map/ppermute | solution.py:209
  170.6 12.4 %collective-permute-done.19.refs_5_.rest_2_ = bf16[8,48,1024]{2,1,0:T(8,128)(2,1)S(1)} collective-permute-done((bf16[8,48,1024]{2,1,0:T(8,128)(2,1)}, bf16[8,48,1024]{2,1,0:T(8,128)(2,1)S(1)}, u32[]{:S(2)}, u32[]{:S(2)}) %collective-permute-start.19) | collective-permute-done | bytes 786464 | tf_op jit(solution)/shard_map/ppermute | solution.py:209
  183.0 7.2 %collective-permute-done.20.refs_6_.rest_3_ = bf16[8,48,1024]{2,1,0:T(8,128)(2,1)} collective-permute-done((bf16[8,48,1024]{2,1,0:T(8,128)(2,1)}, bf16[8,48,1024]{2,1,0:T(8,128)(2,1)}, u32[]{:S(2)}, u32[]{:S(2)}) %collective-permute-start.20) | collective-permute-done | bytes 786464 | tf_op jit(solution)/shard_map/ppermute | solution.py:209
  191.2 1.9 collective-permute-start.21
  193.1 1.4 collective-permute-start.22
  194.7 2.3 %collect.3.rest_4_ = bf16[16,128,1024]{2,1,0:T(8,128)(2,1)} custom-call(s32[32]{0:T(128)S(1)} %copy-done.13, bf16[16,128,1024]{2,1,0:T(8,128)(2,1)S(1)} %copy-done.1, bf16[8,32,1024]{2,1,0:T(8,128)(2,1)S(1)} %copy-done.11, bf16[8,32,1024]{2,1,0:T(8,128)(2,1)S(1)} %copy-done.3, bf16[8,32,1024]{2,1,0:T(8,128)(2,1)S(1)} %copy-done.5, ...), custom_call_target="tpu_custom_call" | custom-call | bytes 8388608 | tf_op jit(solution)/shard_map/collect/pallas_call | solution.py:149
  197.0 3.3 %collect.4.rest_4_ = bf16[16,128,1024]{2,1,0:T(8,128)(2,1)} custom-call(s32[32]{0:T(128)S(1)} %copy-done.13, bf16[16,128,1024]{2,1,0:T(8,128)(2,1)S(1)} %copy-done.1, bf16[8,48,1024]{2,1,0:T(8,128)(2,1)S(1)} %copy-done.9, bf16[8,48,1024]{2,1,0:T(8,128)(2,1)S(1)} %collective-permute-done.18.refs_4_.rest_1_, ...), custom_call_target="tpu_custom_call", output_to_operand_aliasing={{}: (6, {})} | custom-call | bytes 12582912 | tf_op jit(solution)/shard_map/collect/pallas_call | solution.py:149
  200.3 3.0 %collective-permute-done.21.rest_1_ = bf16[8,48,1024]{2,1,0:T(8,128)(2,1)S(1)} collective-permute-done((bf16[8,48,1024]{2,1,0:T(8,128)(2,1)S(1)}, bf16[8,48,1024]{2,1,0:T(8,128)(2,1)S(1)}, u32[]{:S(2)}, u32[]{:S(2)}) %collective-permute-start.21) | collective-permute-done | bytes 786464 | tf_op jit(solution)/shard_map/ppermute | solution.py:209
  203.3 9.6 %collective-permute-done.22.rest_2_ = bf16[8,48,1024]{2,1,0:T(8,128)(2,1)S(1)} collective-permute-done((bf16[8,48,1024]{2,1,0:T(8,128)(2,1)S(1)}, bf16[8,48,1024]{2,1,0:T(8,128)(2,1)S(1)}, u32[]{:S(2)}, u32[]{:S(2)}) %collective-permute-start.22) | collective-permute-done | bytes 786464 | tf_op jit(solution)/shard_map/ppermute | solution.py:209
  212.8 1.0 collective-permute-done.23.rest_3_
  213.8 2.7 %collect.5 = bf16[16,128,1024]{2,1,0:T(8,128)(2,1)} custom-call(s32[32]{0:T(128)S(1)} %copy-done.13, bf16[16,128,1024]{2,1,0:T(8,128)(2,1)S(1)} %copy-done.1, bf16[8,48,1024]{2,1,0:T(8,128)(2,1)S(1)} %get-tuple-element.63.rest_0_, bf16[8,48,1024]{2,1,0:T(8,128)(2,1)S(1)} %collective-permute-done.21.rest_1_, ...), custom_call_target="tpu_custom_call", output_to_operand_aliasing={{}: (6, {})} | custom-call | bytes 12582912 | tf_op jit(solution)/shard_map/collect/pallas_call | solution.py:149
  (59 shorter events, 8.5 us)
Async XLA Ops:
  0.6 8.8 %copy-start = (f32[16,1024]{1,0:T(8,128)S(1)}, f32[16,1024]{1,0:T(8,128)}, u32[]{:S(2)}) copy-start(f32[16,1024]{1,0:T(8,128)} %param.5) | copy-start | bytes 196612
  0.6 5.5 %copy-start.14 = (s32[16,1]{0,1:T(1,128)S(1)}, s32[16,1]{0,1:T(1,128)}, u32[]{:S(2)}) copy-start(s32[16,1]{0,1:T(1,128)} %param.7) | copy-start | bytes 196
  0.7 55.2 %all-to-all-start = ((bf16[8,2,128,1024]{3,2,1,0:T(8,128)(2,1)}), bf16[8,2,128,1024]{3,2,1,0:T(8,128)(2,1)}, u32[]{:S(2)}, u32[]{:S(2)}) async-start(bf16[8,2,128,1024]{3,2,1,0:T(8,128)(2,1)} %bitcast.28), calls=%async_computation | async-start | bytes 8388608 | tf_op jit(solution)/shard_map/all_to_all | solution.py:252
  6.1 3.6 %collective-permute-start.2 = (s32[16]{0:T(128)S(1)}, s32[16]{0:T(128)S(1)}, u32[]{:S(2)}, u32[]{:S(2)}) collective-permute-start(s32[16]{0:T(128)S(1)} %bitcast.21), channel_id=1, source_target_pairs={{0,96},{1,25},{2,98},{3,27},{4,100},{5,29},{6,102},{7,31},{8,104},... | collective-permute-start | bytes 200 | tf_op jit(solution)/shard_map/ppermute | solution.py:209
  6.7 5.0 %collective-permute-start.1 = (s32[16]{0:T(128)S(1)}, s32[16]{0:T(128)S(1)}, u32[]{:S(2)}, u32[]{:S(2)}) collective-permute-start(s32[16]{0:T(128)S(1)} %bitcast.22), channel_id=1, source_target_pairs={{0,64},{1,17},{2,66},{3,19},{4,68},{5,21},{6,70},{7,23},{8,72},{9,... | collective-permute-start | bytes 200 | tf_op jit(solution)/shard_map/ppermute | solution.py:209
  9.5 3.5 %collective-permute-start = (s32[16]{0:T(128)S(1)}, s32[16]{0:T(128)S(1)}, u32[]{:S(2)}, u32[]{:S(2)}) collective-permute-start(s32[16]{0:T(128)S(1)} %bitcast.23), channel_id=1, source_target_pairs={{0,32},{1,9},{2,34},{3,11},{4,36},{5,13},{6,38},{7,15},{8,40},{9,1... | collective-permute-start | bytes 200 | tf_op jit(solution)/shard_map/ppermute | solution.py:209
  13.0 5.2 %collective-permute-start.4 = (s32[4,16]{1,0:T(4,128)S(1)}, s32[4,16]{1,0:T(4,128)S(1)}, u32[]{:S(2)}, u32[]{:S(2)}) collective-permute-start(s32[4,16]{1,0:T(4,128)S(1)} %get-tuple-element.71), channel_id=1, source_target_pairs={{0,16},{1,65},{2,18},{3,67},{4,20},{5,69},{6,22},{7,71},{8,24},{9,... | collective-permute-start | bytes 776 | tf_op jit(solution)/shard_map/ppermute | solution.py:209
  13.4 4.8 %collective-permute-start.3 = (s32[4,16]{1,0:T(4,128)S(1)}, s32[4,16]{1,0:T(4,128)S(1)}, u32[]{:S(2)}, u32[]{:S(2)}) collective-permute-start(s32[4,16]{1,0:T(4,128)S(1)} %get-tuple-element.71), channel_id=1, source_target_pairs={{0,8},{1,33},{2,10},{3,35},{4,12},{5,37},{6,14},{7,39},{8,16},{9,4... | collective-permute-start | bytes 776 | tf_op jit(solution)/shard_map/ppermute | solution.py:209
  15.6 3.7 %collective-permute-start.5 = (s32[4,16]{1,0:T(4,128)S(1)}, s32[4,16]{1,0:T(4,128)S(1)}, u32[]{:S(2)}, u32[]{:S(2)}) collective-permute-start(s32[4,16]{1,0:T(4,128)S(1)} %get-tuple-element.71), channel_id=1, source_target_pairs={{0,24},{1,97},{2,26},{3,99},{4,28},{5,101},{6,30},{7,103},{8,0},{9... | collective-permute-start | bytes 776 | tf_op jit(solution)/shard_map/ppermute | solution.py:209
  65.2 19.5 %all-to-all-start.1 = ((bf16[8,2,32,1024]{3,2,1,0:T(8,128)(2,1)}), bf16[8,2,32,1024]{3,2,1,0:T(8,128)(2,1)S(1)}, u32[]{:S(2)}, u32[]{:S(2)}) async-start(bf16[8,2,32,1024]{3,2,1,0:T(8,128)(2,1)} %sweeps.3), calls=%async_computation.1 | async-start | bytes 2097152 | tf_op jit(solution)/shard_map/all_to_all | solution.py:261
  69.0 19.3 %copy-start.12 = (s32[4]{0:T(128)S(1)}, s32[4]{0:T(128)}, u32[]{:S(2)}) copy-start(s32[4]{0:T(128)} %pad_add_fusion.2.place_ref) | copy-start | bytes 52
  84.7 26.7 %all-to-all-start.3 = ((bf16[8,2,48,1024]{3,2,1,0:T(8,128)(2,1)}), bf16[8,2,48,1024]{3,2,1,0:T(8,128)(2,1)S(1)}, u32[]{:S(2)}, u32[]{:S(2)}) async-start(bf16[8,2,48,1024]{3,2,1,0:T(8,128)(2,1)} %sweeps.4.rest_0_), calls=%async_computation.3 | async-start | bytes 3145728 | tf_op jit(solution)/shard_map/all_to_all | solution.py:261
  89.8 15.9 %collective-permute-start.6 = (bf16[8,32,1024]{2,1,0:T(8,128)(2,1)S(1)}, bf16[8,32,1024]{2,1,0:T(8,128)(2,1)S(1)}, u32[]{:S(2)}, u32[]{:S(2)}) collective-permute-start(bf16[8,32,1024]{2,1,0:T(8,128)(2,1)S(1)} %get-tuple-element.41), channel_id=1, source_target_pairs={{0,32},{1,9},{2,34},{3,11},{4,36},{5,13},{6,38},{7,15},{8,40},{9,1... | collective-permute-start | bytes 1572872 | tf_op jit(solution)/shard_map/ppermute | solution.py:209
  91.0 14.6 %collective-permute-start.7 = (bf16[8,32,1024]{2,1,0:T(8,128)(2,1)S(1)}, bf16[8,32,1024]{2,1,0:T(8,128)(2,1)S(1)}, u32[]{:S(2)}, u32[]{:S(2)}) collective-permute-start(bf16[8,32,1024]{2,1,0:T(8,128)(2,1)S(1)} %get-tuple-element.42), channel_id=1, source_target_pairs={{0,64},{1,17},{2,66},{3,19},{4,68},{5,21},{6,70},{7,23},{8,72},{9,... | collective-permute-start | bytes 1572872 | tf_op jit(solution)/shard_map/ppermute | solution.py:209
  91.8 14.9 %collective-permute-start.8 = (bf16[8,32,1024]{2,1,0:T(8,128)(2,1)S(1)}, bf16[8,32,1024]{2,1,0:T(8,128)(2,1)S(1)}, u32[]{:S(2)}, u32[]{:S(2)}) collective-permute-start(bf16[8,32,1024]{2,1,0:T(8,128)(2,1)S(1)} %get-tuple-element.43), channel_id=1, source_target_pairs={{0,96},{1,25},{2,98},{3,27},{4,100},{5,29},{6,102},{7,31},{8,104},... | collective-permute-start | bytes 1572872 | tf_op jit(solution)/shard_map/ppermute | solution.py:209
  107.7 0.8 copy-start.10
  108.5 0.8 copy-start.16
  109.3 0.8 copy-start.15
  110.1 14.5 %collective-permute-start.12 = (bf16[8,32,1024]{2,1,0:T(8,128)(2,1)}, bf16[8,32,1024]{2,1,0:T(8,128)(2,1)S(1)}, u32[]{:S(2)}, u32[]{:S(2)}) collective-permute-start(bf16[8,32,1024]{2,1,0:T(8,128)(2,1)} %get-tuple-element.50), channel_id=1, source_target_pairs={{0,8},{1,33},{2,10},{3,35},{4,12},{5,37},{6,14},{7,39},{8,16},{9,4... | collective-permute-start | bytes 1572872 | tf_op jit(solution)/shard_map/ppermute | solution.py:209
  114.6 31.7 %collective-permute-start.9 = (bf16[8,48,1024]{2,1,0:T(8,128)(2,1)}, bf16[8,48,1024]{2,1,0:T(8,128)(2,1)}, u32[]{:S(2)}, u32[]{:S(2)}) collective-permute-start(bf16[8,48,1024]{2,1,0:T(8,128)(2,1)} %get-tuple-element.47), channel_id=1, source_target_pairs={{0,32},{1,9},{2,34},{3,11},{4,36},{5,13},{6,38},{7,15},{8,40},{9,1... | collective-permute-start | bytes 2359304 | tf_op jit(solution)/shard_map/ppermute | solution.py:209
  115.7 30.6 %collective-permute-start.10 = (bf16[8,48,1024]{2,1,0:T(8,128)(2,1)}, bf16[8,48,1024]{2,1,0:T(8,128)(2,1)}, u32[]{:S(2)}, u32[]{:S(2)}) collective-permute-start(bf16[8,48,1024]{2,1,0:T(8,128)(2,1)} %get-tuple-element.48), channel_id=1, source_target_pairs={{0,64},{1,17},{2,66},{3,19},{4,68},{5,21},{6,70},{7,23},{8,72},{9,... | collective-permute-start | bytes 2359304 | tf_op jit(solution)/shard_map/ppermute | solution.py:209
  117.2 30.5 %collective-permute-start.11 = (bf16[8,48,1024]{2,1,0:T(8,128)(2,1)}, bf16[8,48,1024]{2,1,0:T(8,128)(2,1)}, u32[]{:S(2)}, u32[]{:S(2)}) collective-permute-start(bf16[8,48,1024]{2,1,0:T(8,128)(2,1)} %get-tuple-element.49), channel_id=1, source_target_pairs={{0,96},{1,25},{2,98},{3,27},{4,100},{5,29},{6,102},{7,31},{8,104},... | collective-permute-start | bytes 2359304 | tf_op jit(solution)/shard_map/ppermute | solution.py:209
  119.2 36.1 %all-to-all-start.2 = ((bf16[8,2,48,1024]{3,2,1,0:T(8,128)(2,1)}), bf16[8,2,48,1024]{3,2,1,0:T(8,128)(2,1)S(1)}, u32[]{:S(2)}, u32[]{:S(2)}) async-start(bf16[8,2,48,1024]{3,2,1,0:T(8,128)(2,1)} %sweeps.5.refs_4_), calls=%async_computation.2 | async-start | bytes 3145728 | tf_op jit(solution)/shard_map/all_to_all | solution.py:261
  123.9 16.6 %collective-permute-start.13 = (bf16[8,32,1024]{2,1,0:T(8,128)(2,1)}, bf16[8,32,1024]{2,1,0:T(8,128)(2,1)S(1)}, u32[]{:S(2)}, u32[]{:S(2)}) collective-permute-start(bf16[8,32,1024]{2,1,0:T(8,128)(2,1)} %copy-done.16), channel_id=1, source_target_pairs={{0,16},{1,65},{2,18},{3,67},{4,20},{5,69},{6,22},{7,71},{8,24},{9,... | collective-permute-start | bytes 1572872 | tf_op jit(solution)/shard_map/ppermute | solution.py:209
  124.6 26.2 %copy-start.2 = (bf16[8,32,1024]{2,1,0:T(8,128)(2,1)}, bf16[8,32,1024]{2,1,0:T(8,128)(2,1)S(1)}, u32[]{:S(2)}) copy-start(bf16[8,32,1024]{2,1,0:T(8,128)(2,1)S(1)} %collective-permute-done.12.refs_4_.rest_1_) | copy-start | bytes 1572868
  124.6 21.6 %collective-permute-start.14 = (bf16[8,32,1024]{2,1,0:T(8,128)(2,1)}, bf16[8,32,1024]{2,1,0:T(8,128)(2,1)S(1)}, u32[]{:S(2)}, u32[]{:S(2)}) collective-permute-start(bf16[8,32,1024]{2,1,0:T(8,128)(2,1)} %copy-done.15), channel_id=1, source_target_pairs={{0,24},{1,97},{2,26},{3,99},{4,28},{5,101},{6,30},{7,103},{8,0},{9... | collective-permute-start | bytes 1572872 | tf_op jit(solution)/shard_map/ppermute | solution.py:209
  140.6 13.3 %copy-start.4 = (bf16[8,32,1024]{2,1,0:T(8,128)(2,1)}, bf16[8,32,1024]{2,1,0:T(8,128)(2,1)S(1)}, u32[]{:S(2)}) copy-start(bf16[8,32,1024]{2,1,0:T(8,128)(2,1)S(1)} %collective-permute-done.13.refs_5_.rest_2_) | copy-start | bytes 1572868
  146.2 7.7 %copy-start.6 = (bf16[8,32,1024]{2,1,0:T(8,128)(2,1)}, bf16[8,32,1024]{2,1,0:T(8,128)(2,1)S(1)}, u32[]{:S(2)}) copy-start(bf16[8,32,1024]{2,1,0:T(8,128)(2,1)S(1)} %collective-permute-done.14.refs_6_.rest_3_) | copy-start | bytes 1572868
  150.8 0.9 copy-start.8
  151.7 14.3 %collective-permute-start.18 = (bf16[8,48,1024]{2,1,0:T(8,128)(2,1)}, bf16[8,48,1024]{2,1,0:T(8,128)(2,1)S(1)}, u32[]{:S(2)}, u32[]{:S(2)}) collective-permute-start(bf16[8,48,1024]{2,1,0:T(8,128)(2,1)} %get-tuple-element.60), channel_id=1, source_target_pairs={{0,8},{1,33},{2,10},{3,35},{4,12},{5,37},{6,14},{7,39},{8,16},{9,4... | collective-permute-start | bytes 2359304 | tf_op jit(solution)/shard_map/ppermute | solution.py:209
  151.9 31.1 %collective-permute-start.19 = (bf16[8,48,1024]{2,1,0:T(8,128)(2,1)}, bf16[8,48,1024]{2,1,0:T(8,128)(2,1)S(1)}, u32[]{:S(2)}, u32[]{:S(2)}) collective-permute-start(bf16[8,48,1024]{2,1,0:T(8,128)(2,1)} %get-tuple-element.61), channel_id=1, source_target_pairs={{0,16},{1,65},{2,18},{3,67},{4,20},{5,69},{6,22},{7,71},{8,24},{9,... | collective-permute-start | bytes 2359304 | tf_op jit(solution)/shard_map/ppermute | solution.py:209
  153.9 36.3 %collective-permute-start.20 = (bf16[8,48,1024]{2,1,0:T(8,128)(2,1)}, bf16[8,48,1024]{2,1,0:T(8,128)(2,1)}, u32[]{:S(2)}, u32[]{:S(2)}) collective-permute-start(bf16[8,48,1024]{2,1,0:T(8,128)(2,1)} %get-tuple-element.62), channel_id=1, source_target_pairs={{0,24},{1,97},{2,26},{3,99},{4,28},{5,101},{6,30},{7,103},{8,0},{9... | collective-permute-start | bytes 2359304 | tf_op jit(solution)/shard_map/ppermute | solution.py:209
  155.4 39.3 %copy-start.7 = (bf16[8,32,1024]{2,1,0:T(8,128)(2,1)S(1)}, bf16[8,32,1024]{2,1,0:T(8,128)(2,1)}, u32[]{:S(2)}) copy-start(bf16[8,32,1024]{2,1,0:T(8,128)(2,1)} %copy-done.6) | copy-start | bytes 1572868
  155.4 39.3 %copy-start.11 = (bf16[8,32,1024]{2,1,0:T(8,128)(2,1)S(1)}, bf16[8,32,1024]{2,1,0:T(8,128)(2,1)}, u32[]{:S(2)}) copy-start(bf16[8,32,1024]{2,1,0:T(8,128)(2,1)} %copy-done.10) | copy-start | bytes 1572868
  157.7 37.0 %copy-start.1 = (bf16[16,128,1024]{2,1,0:T(8,128)(2,1)S(1)}, bf16[16,128,1024]{2,1,0:T(8,128)(2,1)}, u32[]{:S(2)}) copy-start(bf16[16,128,1024]{2,1,0:T(8,128)(2,1)} %other_ref.5) | copy-start | bytes 12582916
  157.7 37.0 %copy-start.3 = (bf16[8,32,1024]{2,1,0:T(8,128)(2,1)S(1)}, bf16[8,32,1024]{2,1,0:T(8,128)(2,1)}, u32[]{:S(2)}) copy-start(bf16[8,32,1024]{2,1,0:T(8,128)(2,1)} %copy-done.2) | copy-start | bytes 1572868
  157.7 37.0 %copy-start.5 = (bf16[8,32,1024]{2,1,0:T(8,128)(2,1)S(1)}, bf16[8,32,1024]{2,1,0:T(8,128)(2,1)}, u32[]{:S(2)}) copy-start(bf16[8,32,1024]{2,1,0:T(8,128)(2,1)} %copy-done.4) | copy-start | bytes 1572868
  157.7 37.0 %copy-start.13 = (s32[32]{0:T(128)S(1)}, s32[32]{0:T(128)}, u32[]{:S(2)}) copy-start(s32[32]{0:T(128)} %find.1.ids_ref) | copy-start | bytes 388
  157.7 32.5 %collective-permute-start.15 = (bf16[8,48,1024]{2,1,0:T(8,128)(2,1)S(1)}, bf16[8,48,1024]{2,1,0:T(8,128)(2,1)S(1)}, u32[]{:S(2)}, u32[]{:S(2)}) collective-permute-start(bf16[8,48,1024]{2,1,0:T(8,128)(2,1)S(1)} %get-tuple-element.57), channel_id=1, source_target_pairs={{0,32},{1,9},{2,34},{3,11},{4,36},{5,13},{6,38},{7,15},{8,40},{9,1... | collective-permute-start | bytes 2359304 | tf_op jit(solution)/shard_map/ppermute | solution.py:209
  161.0 29.3 %collective-permute-start.16 = (bf16[8,48,1024]{2,1,0:T(8,128)(2,1)S(1)}, bf16[8,48,1024]{2,1,0:T(8,128)(2,1)S(1)}, u32[]{:S(2)}, u32[]{:S(2)}) collective-permute-start(bf16[8,48,1024]{2,1,0:T(8,128)(2,1)S(1)} %get-tuple-element.58), channel_id=1, source_target_pairs={{0,64},{1,17},{2,66},{3,19},{4,68},{5,21},{6,70},{7,23},{8,72},{9,... | collective-permute-start | bytes 2359304 | tf_op jit(solution)/shard_map/ppermute | solution.py:209
  166.0 25.1 %collective-permute-start.17 = (bf16[8,48,1024]{2,1,0:T(8,128)(2,1)S(1)}, bf16[8,48,1024]{2,1,0:T(8,128)(2,1)S(1)}, u32[]{:S(2)}, u32[]{:S(2)}) collective-permute-start(bf16[8,48,1024]{2,1,0:T(8,128)(2,1)S(1)} %get-tuple-element.59), channel_id=1, source_target_pairs={{0,96},{1,25},{2,98},{3,27},{4,100},{5,29},{6,102},{7,31},{8,104},... | collective-permute-start | bytes 2359304 | tf_op jit(solution)/shard_map/ppermute | solution.py:209
  191.2 12.1 %collective-permute-start.21 = (bf16[8,48,1024]{2,1,0:T(8,128)(2,1)S(1)}, bf16[8,48,1024]{2,1,0:T(8,128)(2,1)S(1)}, u32[]{:S(2)}, u32[]{:S(2)}) collective-permute-start(bf16[8,48,1024]{2,1,0:T(8,128)(2,1)S(1)} %get-tuple-element.64), channel_id=1, source_target_pairs={{0,8},{1,33},{2,10},{3,35},{4,12},{5,37},{6,14},{7,39},{8,16},{9,4... | collective-permute-start | bytes 2359304 | tf_op jit(solution)/shard_map/ppermute | solution.py:209
  193.1 19.8 %collective-permute-start.22 = (bf16[8,48,1024]{2,1,0:T(8,128)(2,1)S(1)}, bf16[8,48,1024]{2,1,0:T(8,128)(2,1)S(1)}, u32[]{:S(2)}, u32[]{:S(2)}) collective-permute-start(bf16[8,48,1024]{2,1,0:T(8,128)(2,1)S(1)} %get-tuple-element.65), channel_id=1, source_target_pairs={{0,16},{1,65},{2,18},{3,67},{4,20},{5,69},{6,22},{7,71},{8,24},{9,... | collective-permute-start | bytes 2359304 | tf_op jit(solution)/shard_map/ppermute | solution.py:209
  194.4 19.4 %collective-permute-start.23 = (bf16[8,48,1024]{2,1,0:T(8,128)(2,1)S(1)}, bf16[8,48,1024]{2,1,0:T(8,128)(2,1)S(1)}, u32[]{:S(2)}, u32[]{:S(2)}) collective-permute-start(bf16[8,48,1024]{2,1,0:T(8,128)(2,1)S(1)} %get-tuple-element.66), channel_id=1, source_target_pairs={{0,24},{1,97},{2,26},{3,99},{4,28},{5,101},{6,30},{7,103},{8,0},{9... | collective-permute-start | bytes 2359304 | tf_op jit(solution)/shard_map/ppermute | solution.py:209
  194.7 2.3 %copy-start.9 = (bf16[8,48,1024]{2,1,0:T(8,128)(2,1)S(1)}, bf16[8,48,1024]{2,1,0:T(8,128)(2,1)}, u32[]{:S(2)}) copy-start(bf16[8,48,1024]{2,1,0:T(8,128)(2,1)} %copy-done.8) | copy-start | bytes 2359300

commit v4 on v3

--- a/solution.py
+++ b/solution.py
@@ -10,6 +10,7 @@
 CAP = 2
 ITERS = 6
 SIDE = 4
+PARTS = 4
 SWEEP_MIB = 24
 PACK_MIB = 12
 GROUP_MIB = 12
@@ -125,10 +126,15 @@
 def collect_kernel(first, rows, ids_ref, other_ref, *rest):
     pieces, (out_ref, total, staged, sems) = rest[:SIDE], rest[-4:]
     window = slice(first, first + rows)
-    read = pltpu.make_async_copy(other_ref.at[:, window], staged, sems.at[0])
-    read.start()
-    read.wait()
-    total[...] = staged[...].astype(jnp.float32)
+    share = staged.shape[0] // PARTS
+    spans = [slice(part * share, part * share + share) for part in range(PARTS)]
+    reads = [pltpu.make_async_copy(other_ref.at[q, window], staged.at[q], sems.at[0, i]) for i, q in enumerate(spans)]
+    writes = [pltpu.make_async_copy(staged.at[q], out_ref.at[q, window], sems.at[1, i]) for i, q in enumerate(spans)]
+    for read in reads:
+        read.start()
+    for read, span in zip(reads, spans):
+        read.wait()
+        total[span] = staged[span].astype(jnp.float32)
     for two in range(SIDE):
         for at in range(SIDE * CAP):
             target = ids_ref[two * SIDE * CAP + at]
@@ -137,10 +143,11 @@
             def _():
                 total[target] += pieces[two][at].astype(jnp.float32)
 
-    staged[...] = total[...].astype(jnp.bfloat16)
-    write = pltpu.make_async_copy(staged, out_ref.at[:, window], sems.at[1])
-    write.start()
-    write.wait()
+    for write, span in zip(writes, spans):
+        staged[span] = total[span].astype(jnp.bfloat16)
+        write.start()
+    for write in writes:
+        write.wait()
 
 
 def collect(ids, other, pieces, crossed, first, earlier=()):
@@ -154,7 +161,7 @@
         scratch_shapes=[
             pltpu.VMEM((q_local, rows, width), jnp.float32),
             pltpu.VMEM((q_local, rows, width), jnp.bfloat16),
-            pltpu.SemaphoreType.DMA((2,)),
+            pltpu.SemaphoreType.DMA((2, PARTS)),
         ],
         input_output_aliases={2 + SIDE: 0} if crossed else {},
         compiler_params=params(16),

time: 220 us -> 220 us (level)
  no operation moved by 1% of the time
where the time goes in v4:
time: 220 us; the launch traced here: 217 us
  waiting for transfers between devices  102 us (46%)
  Pallas kernels  59.1 us (27%)
  starting transfers between devices  49.8 us (23%)
  local copies, waits for them, and re-layouts  3.38 us (2%)
    ppermute x24, waiting for transfers between devices, shift(): return lax.ppermute(value, ('boson', 'row'), pairs)  68.1 us
    pallas_call x3, Pallas kernels, sweeps(): pl.pallas_call(functools.partial(sweep_kernel, first, rows), in_specs=[HB...  34.6 us
    ppermute x24, starting transfers between devices, shift(): return lax.ppermute(value, ('boson', 'row'), pairs)  32.3 us
    all_to_all x1, waiting for transfers between devices, local(): lax.all_to_all(vertex.reshape(n_row, mine, freq, width), 'row', split_axi...  30.9 us
    all_to_all x3, starting transfers between devices, back(): lax.all_to_all(solved, 'row', split_axis=0, concat_axis=0, tiled=True)  12 us
    pallas_call x3, Pallas kernels, collect(): pl.pallas_call(functools.partial(collect_kernel, first, rows), in_specs=[...  8.33 us
    pallas_call x3, Pallas kernels, pack(): pl.pallas_call(functools.partial(pack_kernel, first, rows), in_specs=[SME...  6.96 us
    all_to_all x1, starting transfers between devices, local(): lax.all_to_all(vertex.reshape(n_row, mine, freq, width), 'row', split_axi...  5.46 us
  transfers between devices with their start and end apart: 28, of which 18 were waited for; matrix products, arithmetic and copies ran while one was open for 1% of the time, Pallas kernels for 22%

profile of v4, /device:TPU:20, one launch (start us, length us, event | category | flops | bytes accessed | tf_op | source)
XLA Modules:
  0.0 216.8 jit_solution(3370194386053840623)
XLA Ops:
  0.7 5.5 %all-to-all-start = ((bf16[8,2,128,1024]{3,2,1,0:T(8,128)(2,1)}), bf16[8,2,128,1024]{3,2,1,0:T(8,128)(2,1)}, u32[]{:S(2)}, u32[]{:S(2)}) async-start(bf16[8,2,128,1024]{3,2,1,0:T(8,128)(2,1)} %bitcast.28), calls=%async_computation | async-start | bytes 8388608 | tf_op jit(solution)/shard_map/all_to_all | solution.py:259
  6.7 2.7 %collective-permute-start.1 = (s32[16]{0:T(128)S(1)}, s32[16]{0:T(128)S(1)}, u32[]{:S(2)}, u32[]{:S(2)}) collective-permute-start(s32[16]{0:T(128)S(1)} %bitcast.22), channel_id=1, source_target_pairs={{0,64},{1,17},{2,66},{3,19},{4,68},{5,21},{6,70},{7,23},{8,72},{9,... | collective-permute-start | bytes 200 | tf_op jit(solution)/shard_map/ppermute | solution.py:216
  9.7 2.0 collective-permute-done.1
  11.8 1.2 collective-permute-done
  13.4 2.2 %collective-permute-start.3 = (s32[4,16]{1,0:T(4,128)S(1)}, s32[4,16]{1,0:T(4,128)S(1)}, u32[]{:S(2)}, u32[]{:S(2)}) collective-permute-start(s32[4,16]{1,0:T(4,128)S(1)} %get-tuple-element.71), channel_id=1, source_target_pairs={{0,8},{1,33},{2,10},{3,35},{4,12},{5,37},{6,14},{7,39},{8,16},{9,4... | collective-permute-start | bytes 776 | tf_op jit(solution)/shard_map/ppermute | solution.py:216
  16.5 1.7 collective-permute-done.4
  18.2 1.2 collective-permute-done.5
  20.0 5.0 %find.1.ids_ref = s32[32]{0:T(128)} custom-call(s32[4]{0:T(128)} %pad_add_fusion.2.place_ref, s32[4,4,16]{2,1,0:T(4,128)} %pad_add_fusion.everyone_ref), custom_call_target="tpu_custom_call" | custom-call | tf_op jit(solution)/shard_map/find/pallas_call | solution.py:195
  25.0 30.9 %all-to-all-done.vertex_ref = bf16[8,2,128,1024]{3,2,1,0:T(8,128)(2,1)} async-done(((bf16[8,2,128,1024]{3,2,1,0:T(8,128)(2,1)}), bf16[8,2,128,1024]{3,2,1,0:T(8,128)(2,1)}, u32[]{:S(2)}, u32[]{:S(2)}) %all-to-all-start) | async-done | bytes 4194336 | tf_op jit(solution)/shard_map/all_to_all | solution.py:259
  55.9 9.3 %sweeps.3 = bf16[8,2,32,1024]{3,2,1,0:T(8,128)(2,1)} custom-call(bf16[8,2,128,1024]{3,2,1,0:T(8,128)(2,1)} %all-to-all-done.vertex_ref, f32[2,1024]{1,0:T(2,128)S(1)} %constant_dynamic-slice_fusion.bubble_ref), custom_call_target="tpu_custom_call" | custom-call | flops 6442450944 | bytes 4194304 | tf_op jit(solution)/shard_map/sweeps/pallas_call | solution.py:62
  65.2 3.8 %all-to-all-start.1 = ((bf16[8,2,32,1024]{3,2,1,0:T(8,128)(2,1)}), bf16[8,2,32,1024]{3,2,1,0:T(8,128)(2,1)S(1)}, u32[]{:S(2)}, u32[]{:S(2)}) async-start(bf16[8,2,32,1024]{3,2,1,0:T(8,128)(2,1)} %sweeps.3), calls=%async_computation.1 | async-start | bytes 2097152 | tf_op jit(solution)/shard_map/all_to_all | solution.py:268
  69.0 12.6 %sweeps.4.rest_0_ = bf16[8,2,48,1024]{3,2,1,0:T(8,128)(2,1)} custom-call(bf16[8,2,128,1024]{3,2,1,0:T(8,128)(2,1)} %all-to-all-done.vertex_ref, f32[2,1024]{1,0:T(2,128)S(1)} %constant_dynamic-slice_fusion.bubble_ref), custom_call_target="tpu_custom_call" | custom-call | flops 9663676416 | bytes 4194304 | tf_op jit(solution)/shard_map/sweeps/pallas_call | solution.py:62
  81.6 3.1 %all-to-all-done.1 = bf16[8,2,32,1024]{3,2,1,0:T(8,128)(2,1)S(1)} async-done(((bf16[8,2,32,1024]{3,2,1,0:T(8,128)(2,1)}), bf16[8,2,32,1024]{3,2,1,0:T(8,128)(2,1)S(1)}, u32[]{:S(2)}, u32[]{:S(2)}) %all-to-all-start.1) | async-done | bytes 1048608 | tf_op jit(solution)/shard_map/all_to_all | solution.py:268
  84.7 3.6 %all-to-all-start.3 = ((bf16[8,2,48,1024]{3,2,1,0:T(8,128)(2,1)}), bf16[8,2,48,1024]{3,2,1,0:T(8,128)(2,1)S(1)}, u32[]{:S(2)}, u32[]{:S(2)}) async-start(bf16[8,2,48,1024]{3,2,1,0:T(8,128)(2,1)} %sweeps.4.rest_0_), calls=%async_computation.3 | async-start | bytes 3145728 | tf_op jit(solution)/shard_map/all_to_all | solution.py:268
  88.3 1.5 pack.3
  89.8 1.3 collective-permute-start.6
  91.8 1.1 collective-permute-start.8
  93.0 12.7 %sweeps.5.refs_4_ = bf16[8,2,48,1024]{3,2,1,0:T(8,128)(2,1)} custom-call(bf16[8,2,128,1024]{3,2,1,0:T(8,128)(2,1)} %all-to-all-done.vertex_ref, f32[2,1024]{1,0:T(2,128)S(1)} %constant_dynamic-slice_fusion.bubble_ref, f32[8,128]{1,0:T(8,128)S(1)} %get-tuple-element.38.rest_0_), custom_call_target="tpu_custom_call" | custom-call | flops 9663676416 | bytes 4194304 | tf_op jit(solution)/shard_map/sweeps/pallas_call | solution.py:62
  105.7 1.1 collective-permute-done.8.refs_3_
  106.8 0.9 regroup.3
  110.1 1.3 collective-permute-start.12
  111.4 3.1 %pack.4 = (bf16[16,128,1024]{2,1,0:T(8,128)(2,1)}, bf16[8,48,1024]{2,1,0:T(8,128)(2,1)S(1)}, bf16[8,48,1024]{2,1,0:T(8,128)(2,1)}, bf16[8,48,1024]{2,1,0:T(8,128...) custom-call(s32[4]{0:T(128)S(1)} %copy-done.12, s32[16]{0:T(128)S(1)} %bitcast.26, ...), custom_call_target="tpu_custom_call", output_to_operand_aliasing={{0}: (3, {})} | custom-call | bytes 6291456 | tf_op jit(solution)/shard_map/pack/pallas_call | solution.py:112
  114.6 1.1 collective-permute-start.9
  115.7 1.5 collective-permute-start.10
  117.2 2.1 collective-permute-start.11
  119.2 4.7 %all-to-all-start.2 = ((bf16[8,2,48,1024]{3,2,1,0:T(8,128)(2,1)}), bf16[8,2,48,1024]{3,2,1,0:T(8,128)(2,1)S(1)}, u32[]{:S(2)}, u32[]{:S(2)}) async-start(bf16[8,2,48,1024]{3,2,1,0:T(8,128)(2,1)} %sweeps.5.refs_4_), calls=%async_computation.2 | async-start | bytes 3145728 | tf_op jit(solution)/shard_map/all_to_all | solution.py:268
  124.6 1.0 collective-permute-start.14
  125.6 15.0 %collective-permute-done.13.refs_5_.rest_2_ = bf16[8,32,1024]{2,1,0:T(8,128)(2,1)S(1)} collective-permute-done((bf16[8,32,1024]{2,1,0:T(8,128)(2,1)}, bf16[8,32,1024]{2,1,0:T(8,128)(2,1)S(1)}, u32[]{:S(2)}, u32[]{:S(2)}) %collective-permute-start.13) | collective-permute-done | bytes 524320 | tf_op jit(solution)/shard_map/ppermute | solution.py:216
  140.6 5.7 %collective-permute-done.14.refs_6_.rest_3_ = bf16[8,32,1024]{2,1,0:T(8,128)(2,1)S(1)} collective-permute-done((bf16[8,32,1024]{2,1,0:T(8,128)(2,1)}, bf16[8,32,1024]{2,1,0:T(8,128)(2,1)S(1)}, u32[]{:S(2)}, u32[]{:S(2)}) %collective-permute-start.14) | collective-permute-done | bytes 524320 | tf_op jit(solution)/shard_map/ppermute | solution.py:216
  146.2 1.4 collective-permute-done.11.refs_3_
  147.6 3.1 %regroup.4 = (bf16[8,48,1024]{2,1,0:T(8,128)(2,1)S(1)}, bf16[8,48,1024]{2,1,0:T(8,128)(2,1)}, bf16[8,48,1024]{2,1,0:T(8,128)(2,1)}, bf16[8,48,1024]{2,1,0:T(8,128)(2,1)}, f32[8,128]{1,0:T(8,128)S(1)}) custom-call(bf16[8,48,1024]{2,1,0:T(8,128)(2,1)S(1)} %get-tuple-element.46.refs_0_, bf16[8,48,1024]{2,1,0:T(8,128)(2,1)} %collective-permute-done.9.refs_1_, ...), custom_call_target="tpu_custom_call" | custom-call | bytes 6291456 | tf_op jit(solution)/shard_map/regroup/pallas_call | solution.py:229
  150.8 0.9 copy-done.8
  151.9 2.0 collective-permute-start.19
  153.9 1.5 collective-permute-start.20
  155.4 2.3 %pack.5 = (bf16[16,128,1024]{2,1,0:T(8,128)(2,1)}, bf16[8,48,1024]{2,1,0:T(8,128)(2,1)S(1)}, bf16[8,48,1024]{2,1,0:T(8,128)(2,1)S(1)}, bf16[8,48,1024]{2,1,0:T(8...) custom-call(s32[4]{0:T(128)S(1)} %copy-done.12, ...), custom_call_target="tpu_custom_call", output_to_operand_aliasing={{0}: (3, {})} | custom-call | bytes 6291456 | tf_op jit(solution)/shard_map/pack/pallas_call | solution.py:112
  157.7 3.3 %collective-permute-start.15 = (bf16[8,48,1024]{2,1,0:T(8,128)(2,1)S(1)}, bf16[8,48,1024]{2,1,0:T(8,128)(2,1)S(1)}, u32[]{:S(2)}, u32[]{:S(2)}) collective-permute-start(bf16[8,48,1024]{2,1,0:T(8,128)(2,1)S(1)} %get-tuple-element.57), channel_id=1, source_target_pairs={{0,32},{1,9},{2,34},{3,11},{4,36},{5,13},{6,38},{7,15},{8,40},{9,1... | collective-permute-start | bytes 2359304 | tf_op jit(solution)/shard_map/ppermute | solution.py:216
  161.3 4.6 %collective-permute-done.18.refs_4_.rest_1_ = bf16[8,48,1024]{2,1,0:T(8,128)(2,1)S(1)} collective-permute-done((bf16[8,48,1024]{2,1,0:T(8,128)(2,1)}, bf16[8,48,1024]{2,1,0:T(8,128)(2,1)S(1)}, u32[]{:S(2)}, u32[]{:S(2)}) %collective-permute-start.18) | collective-permute-done | bytes 786464 | tf_op jit(solution)/shard_map/ppermute | solution.py:216
  166.0 4.6 %collective-permute-start.17 = (bf16[8,48,1024]{2,1,0:T(8,128)(2,1)S(1)}, bf16[8,48,1024]{2,1,0:T(8,128)(2,1)S(1)}, u32[]{:S(2)}, u32[]{:S(2)}) collective-permute-start(bf16[8,48,1024]{2,1,0:T(8,128)(2,1)S(1)} %get-tuple-element.59), channel_id=1, source_target_pairs={{0,96},{1,25},{2,98},{3,27},{4,100},{5,29},{6,102},{7,31},{8,104},... | collective-permute-start | bytes 2359304 | tf_op jit(solution)/shard_map/ppermute | solution.py:216
  170.6 12.4 %collective-permute-done.19.refs_5_.rest_2_ = bf16[8,48,1024]{2,1,0:T(8,128)(2,1)S(1)} collective-permute-done((bf16[8,48,1024]{2,1,0:T(8,128)(2,1)}, bf16[8,48,1024]{2,1,0:T(8,128)(2,1)S(1)}, u32[]{:S(2)}, u32[]{:S(2)}) %collective-permute-start.19) | collective-permute-done | bytes 786464 | tf_op jit(solution)/shard_map/ppermute | solution.py:216
  183.0 7.2 %collective-permute-done.20.refs_6_.rest_3_ = bf16[8,48,1024]{2,1,0:T(8,128)(2,1)} collective-permute-done((bf16[8,48,1024]{2,1,0:T(8,128)(2,1)}, bf16[8,48,1024]{2,1,0:T(8,128)(2,1)}, u32[]{:S(2)}, u32[]{:S(2)}) %collective-permute-start.20) | collective-permute-done | bytes 786464 | tf_op jit(solution)/shard_map/ppermute | solution.py:216
  191.2 1.9 collective-permute-start.21
  193.1 1.4 collective-permute-start.22
  194.7 2.2 %collect.3.rest_4_ = bf16[16,128,1024]{2,1,0:T(8,128)(2,1)} custom-call(s32[32]{0:T(128)S(1)} %copy-done.13, bf16[16,128,1024]{2,1,0:T(8,128)(2,1)S(1)} %copy-done.1, bf16[8,32,1024]{2,1,0:T(8,128)(2,1)S(1)} %copy-done.11, bf16[8,32,1024]{2,1,0:T(8,128)(2,1)S(1)} %copy-done.3, bf16[8,32,1024]{2,1,0:T(8,128)(2,1)S(1)} %copy-done.5, ...), custom_call_target="tpu_custom_call" | custom-call | bytes 8388608 | tf_op jit(solution)/shard_map/collect/pallas_call | solution.py:156
  196.9 3.4 %collect.4.rest_4_ = bf16[16,128,1024]{2,1,0:T(8,128)(2,1)} custom-call(s32[32]{0:T(128)S(1)} %copy-done.13, bf16[16,128,1024]{2,1,0:T(8,128)(2,1)S(1)} %copy-done.1, bf16[8,48,1024]{2,1,0:T(8,128)(2,1)S(1)} %copy-done.9, bf16[8,48,1024]{2,1,0:T(8,128)(2,1)S(1)} %collective-permute-done.18.refs_4_.rest_1_, ...), custom_call_target="tpu_custom_call", output_to_operand_aliasing={{}: (6, {})} | custom-call | bytes 12582912 | tf_op jit(solution)/shard_map/collect/pallas_call | solution.py:156
  200.3 3.0 %collective-permute-done.21.rest_1_ = bf16[8,48,1024]{2,1,0:T(8,128)(2,1)S(1)} collective-permute-done((bf16[8,48,1024]{2,1,0:T(8,128)(2,1)S(1)}, bf16[8,48,1024]{2,1,0:T(8,128)(2,1)S(1)}, u32[]{:S(2)}, u32[]{:S(2)}) %collective-permute-start.21) | collective-permute-done | bytes 786464 | tf_op jit(solution)/shard_map/ppermute | solution.py:216
  203.3 9.6 %collective-permute-done.22.rest_2_ = bf16[8,48,1024]{2,1,0:T(8,128)(2,1)S(1)} collective-permute-done((bf16[8,48,1024]{2,1,0:T(8,128)(2,1)S(1)}, bf16[8,48,1024]{2,1,0:T(8,128)(2,1)S(1)}, u32[]{:S(2)}, u32[]{:S(2)}) %collective-permute-start.22) | collective-permute-done | bytes 786464 | tf_op jit(solution)/shard_map/ppermute | solution.py:216
  212.8 1.0 collective-permute-done.23.rest_3_
  213.8 2.7 %collect.5 = bf16[16,128,1024]{2,1,0:T(8,128)(2,1)} custom-call(s32[32]{0:T(128)S(1)} %copy-done.13, bf16[16,128,1024]{2,1,0:T(8,128)(2,1)S(1)} %copy-done.1, bf16[8,48,1024]{2,1,0:T(8,128)(2,1)S(1)} %get-tuple-element.63.rest_0_, bf16[8,48,1024]{2,1,0:T(8,128)(2,1)S(1)} %collective-permute-done.21.rest_1_, ...), custom_call_target="tpu_custom_call", output_to_operand_aliasing={{}: (6, {})} | custom-call | bytes 12582912 | tf_op jit(solution)/shard_map/collect/pallas_call | solution.py:156
  (59 shorter events, 8.5 us)
Async XLA Ops:
  0.6 8.8 %copy-start = (f32[16,1024]{1,0:T(8,128)S(1)}, f32[16,1024]{1,0:T(8,128)}, u32[]{:S(2)}) copy-start(f32[16,1024]{1,0:T(8,128)} %param.5) | copy-start | bytes 196612
  0.6 5.5 %copy-start.14 = (s32[16,1]{0,1:T(1,128)S(1)}, s32[16,1]{0,1:T(1,128)}, u32[]{:S(2)}) copy-start(s32[16,1]{0,1:T(1,128)} %param.7) | copy-start | bytes 196
  0.7 55.2 %all-to-all-start = ((bf16[8,2,128,1024]{3,2,1,0:T(8,128)(2,1)}), bf16[8,2,128,1024]{3,2,1,0:T(8,128)(2,1)}, u32[]{:S(2)}, u32[]{:S(2)}) async-start(bf16[8,2,128,1024]{3,2,1,0:T(8,128)(2,1)} %bitcast.28), calls=%async_computation | async-start | bytes 8388608 | tf_op jit(solution)/shard_map/all_to_all | solution.py:259
  6.1 3.6 %collective-permute-start.2 = (s32[16]{0:T(128)S(1)}, s32[16]{0:T(128)S(1)}, u32[]{:S(2)}, u32[]{:S(2)}) collective-permute-start(s32[16]{0:T(128)S(1)} %bitcast.21), channel_id=1, source_target_pairs={{0,96},{1,25},{2,98},{3,27},{4,100},{5,29},{6,102},{7,31},{8,104},... | collective-permute-start | bytes 200 | tf_op jit(solution)/shard_map/ppermute | solution.py:216
  6.7 5.0 %collective-permute-start.1 = (s32[16]{0:T(128)S(1)}, s32[16]{0:T(128)S(1)}, u32[]{:S(2)}, u32[]{:S(2)}) collective-permute-start(s32[16]{0:T(128)S(1)} %bitcast.22), channel_id=1, source_target_pairs={{0,64},{1,17},{2,66},{3,19},{4,68},{5,21},{6,70},{7,23},{8,72},{9,... | collective-permute-start | bytes 200 | tf_op jit(solution)/shard_map/ppermute | solution.py:216
  9.5 3.5 %collective-permute-start = (s32[16]{0:T(128)S(1)}, s32[16]{0:T(128)S(1)}, u32[]{:S(2)}, u32[]{:S(2)}) collective-permute-start(s32[16]{0:T(128)S(1)} %bitcast.23), channel_id=1, source_target_pairs={{0,32},{1,9},{2,34},{3,11},{4,36},{5,13},{6,38},{7,15},{8,40},{9,1... | collective-permute-start | bytes 200 | tf_op jit(solution)/shard_map/ppermute | solution.py:216
  13.0 5.2 %collective-permute-start.4 = (s32[4,16]{1,0:T(4,128)S(1)}, s32[4,16]{1,0:T(4,128)S(1)}, u32[]{:S(2)}, u32[]{:S(2)}) collective-permute-start(s32[4,16]{1,0:T(4,128)S(1)} %get-tuple-element.71), channel_id=1, source_target_pairs={{0,16},{1,65},{2,18},{3,67},{4,20},{5,69},{6,22},{7,71},{8,24},{9,... | collective-permute-start | bytes 776 | tf_op jit(solution)/shard_map/ppermute | solution.py:216
  13.4 4.8 %collective-permute-start.3 = (s32[4,16]{1,0:T(4,128)S(1)}, s32[4,16]{1,0:T(4,128)S(1)}, u32[]{:S(2)}, u32[]{:S(2)}) collective-permute-start(s32[4,16]{1,0:T(4,128)S(1)} %get-tuple-element.71), channel_id=1, source_target_pairs={{0,8},{1,33},{2,10},{3,35},{4,12},{5,37},{6,14},{7,39},{8,16},{9,4... | collective-permute-start | bytes 776 | tf_op jit(solution)/shard_map/ppermute | solution.py:216
  15.6 3.7 %collective-permute-start.5 = (s32[4,16]{1,0:T(4,128)S(1)}, s32[4,16]{1,0:T(4,128)S(1)}, u32[]{:S(2)}, u32[]{:S(2)}) collective-permute-start(s32[4,16]{1,0:T(4,128)S(1)} %get-tuple-element.71), channel_id=1, source_target_pairs={{0,24},{1,97},{2,26},{3,99},{4,28},{5,101},{6,30},{7,103},{8,0},{9... | collective-permute-start | bytes 776 | tf_op jit(solution)/shard_map/ppermute | solution.py:216
  65.2 19.5 %all-to-all-start.1 = ((bf16[8,2,32,1024]{3,2,1,0:T(8,128)(2,1)}), bf16[8,2,32,1024]{3,2,1,0:T(8,128)(2,1)S(1)}, u32[]{:S(2)}, u32[]{:S(2)}) async-start(bf16[8,2,32,1024]{3,2,1,0:T(8,128)(2,1)} %sweeps.3), calls=%async_computation.1 | async-start | bytes 2097152 | tf_op jit(solution)/shard_map/all_to_all | solution.py:268
  69.0 19.3 %copy-start.12 = (s32[4]{0:T(128)S(1)}, s32[4]{0:T(128)}, u32[]{:S(2)}) copy-start(s32[4]{0:T(128)} %pad_add_fusion.2.place_ref) | copy-start | bytes 52
  84.7 26.7 %all-to-all-start.3 = ((bf16[8,2,48,1024]{3,2,1,0:T(8,128)(2,1)}), bf16[8,2,48,1024]{3,2,1,0:T(8,128)(2,1)S(1)}, u32[]{:S(2)}, u32[]{:S(2)}) async-start(bf16[8,2,48,1024]{3,2,1,0:T(8,128)(2,1)} %sweeps.4.rest_0_), calls=%async_computation.3 | async-start | bytes 3145728 | tf_op jit(solution)/shard_map/all_to_all | solution.py:268
  89.8 15.9 %collective-permute-start.6 = (bf16[8,32,1024]{2,1,0:T(8,128)(2,1)S(1)}, bf16[8,32,1024]{2,1,0:T(8,128)(2,1)S(1)}, u32[]{:S(2)}, u32[]{:S(2)}) collective-permute-start(bf16[8,32,1024]{2,1,0:T(8,128)(2,1)S(1)} %get-tuple-element.41), channel_id=1, source_target_pairs={{0,32},{1,9},{2,34},{3,11},{4,36},{5,13},{6,38},{7,15},{8,40},{9,1... | collective-permute-start | bytes 1572872 | tf_op jit(solution)/shard_map/ppermute | solution.py:216
  91.0 14.6 %collective-permute-start.7 = (bf16[8,32,1024]{2,1,0:T(8,128)(2,1)S(1)}, bf16[8,32,1024]{2,1,0:T(8,128)(2,1)S(1)}, u32[]{:S(2)}, u32[]{:S(2)}) collective-permute-start(bf16[8,32,1024]{2,1,0:T(8,128)(2,1)S(1)} %get-tuple-element.42), channel_id=1, source_target_pairs={{0,64},{1,17},{2,66},{3,19},{4,68},{5,21},{6,70},{7,23},{8,72},{9,... | collective-permute-start | bytes 1572872 | tf_op jit(solution)/shard_map/ppermute | solution.py:216
  91.8 14.9 %collective-permute-start.8 = (bf16[8,32,1024]{2,1,0:T(8,128)(2,1)S(1)}, bf16[8,32,1024]{2,1,0:T(8,128)(2,1)S(1)}, u32[]{:S(2)}, u32[]{:S(2)}) collective-permute-start(bf16[8,32,1024]{2,1,0:T(8,128)(2,1)S(1)} %get-tuple-element.43), channel_id=1, source_target_pairs={{0,96},{1,25},{2,98},{3,27},{4,100},{5,29},{6,102},{7,31},{8,104},... | collective-permute-start | bytes 1572872 | tf_op jit(solution)/shard_map/ppermute | solution.py:216
  107.7 0.8 copy-start.10
  108.5 0.8 copy-start.16
  109.3 0.8 copy-start.15
  110.1 14.5 %collective-permute-start.12 = (bf16[8,32,1024]{2,1,0:T(8,128)(2,1)}, bf16[8,32,1024]{2,1,0:T(8,128)(2,1)S(1)}, u32[]{:S(2)}, u32[]{:S(2)}) collective-permute-start(bf16[8,32,1024]{2,1,0:T(8,128)(2,1)} %get-tuple-element.50), channel_id=1, source_target_pairs={{0,8},{1,33},{2,10},{3,35},{4,12},{5,37},{6,14},{7,39},{8,16},{9,4... | collective-permute-start | bytes 1572872 | tf_op jit(solution)/shard_map/ppermute | solution.py:216
  114.6 31.7 %collective-permute-start.9 = (bf16[8,48,1024]{2,1,0:T(8,128)(2,1)}, bf16[8,48,1024]{2,1,0:T(8,128)(2,1)}, u32[]{:S(2)}, u32[]{:S(2)}) collective-permute-start(bf16[8,48,1024]{2,1,0:T(8,128)(2,1)} %get-tuple-element.47), channel_id=1, source_target_pairs={{0,32},{1,9},{2,34},{3,11},{4,36},{5,13},{6,38},{7,15},{8,40},{9,1... | collective-permute-start | bytes 2359304 | tf_op jit(solution)/shard_map/ppermute | solution.py:216
  115.7 30.6 %collective-permute-start.10 = (bf16[8,48,1024]{2,1,0:T(8,128)(2,1)}, bf16[8,48,1024]{2,1,0:T(8,128)(2,1)}, u32[]{:S(2)}, u32[]{:S(2)}) collective-permute-start(bf16[8,48,1024]{2,1,0:T(8,128)(2,1)} %get-tuple-element.48), channel_id=1, source_target_pairs={{0,64},{1,17},{2,66},{3,19},{4,68},{5,21},{6,70},{7,23},{8,72},{9,... | collective-permute-start | bytes 2359304 | tf_op jit(solution)/shard_map/ppermute | solution.py:216
  117.2 30.5 %collective-permute-start.11 = (bf16[8,48,1024]{2,1,0:T(8,128)(2,1)}, bf16[8,48,1024]{2,1,0:T(8,128)(2,1)}, u32[]{:S(2)}, u32[]{:S(2)}) collective-permute-start(bf16[8,48,1024]{2,1,0:T(8,128)(2,1)} %get-tuple-element.49), channel_id=1, source_target_pairs={{0,96},{1,25},{2,98},{3,27},{4,100},{5,29},{6,102},{7,31},{8,104},... | collective-permute-start | bytes 2359304 | tf_op jit(solution)/shard_map/ppermute | solution.py:216
  119.2 36.1 %all-to-all-start.2 = ((bf16[8,2,48,1024]{3,2,1,0:T(8,128)(2,1)}), bf16[8,2,48,1024]{3,2,1,0:T(8,128)(2,1)S(1)}, u32[]{:S(2)}, u32[]{:S(2)}) async-start(bf16[8,2,48,1024]{3,2,1,0:T(8,128)(2,1)} %sweeps.5.refs_4_), calls=%async_computation.2 | async-start | bytes 3145728 | tf_op jit(solution)/shard_map/all_to_all | solution.py:268
  123.9 16.6 %collective-permute-start.13 = (bf16[8,32,1024]{2,1,0:T(8,128)(2,1)}, bf16[8,32,1024]{2,1,0:T(8,128)(2,1)S(1)}, u32[]{:S(2)}, u32[]{:S(2)}) collective-permute-start(bf16[8,32,1024]{2,1,0:T(8,128)(2,1)} %copy-done.16), channel_id=1, source_target_pairs={{0,16},{1,65},{2,18},{3,67},{4,20},{5,69},{6,22},{7,71},{8,24},{9,... | collective-permute-start | bytes 1572872 | tf_op jit(solution)/shard_map/ppermute | solution.py:216
  124.6 26.2 %copy-start.2 = (bf16[8,32,1024]{2,1,0:T(8,128)(2,1)}, bf16[8,32,1024]{2,1,0:T(8,128)(2,1)S(1)}, u32[]{:S(2)}) copy-start(bf16[8,32,1024]{2,1,0:T(8,128)(2,1)S(1)} %collective-permute-done.12.refs_4_.rest_1_) | copy-start | bytes 1572868
  124.6 21.6 %collective-permute-start.14 = (bf16[8,32,1024]{2,1,0:T(8,128)(2,1)}, bf16[8,32,1024]{2,1,0:T(8,128)(2,1)S(1)}, u32[]{:S(2)}, u32[]{:S(2)}) collective-permute-start(bf16[8,32,1024]{2,1,0:T(8,128)(2,1)} %copy-done.15), channel_id=1, source_target_pairs={{0,24},{1,97},{2,26},{3,99},{4,28},{5,101},{6,30},{7,103},{8,0},{9... | collective-permute-start | bytes 1572872 | tf_op jit(solution)/shard_map/ppermute | solution.py:216
  140.6 13.3 %copy-start.4 = (bf16[8,32,1024]{2,1,0:T(8,128)(2,1)}, bf16[8,32,1024]{2,1,0:T(8,128)(2,1)S(1)}, u32[]{:S(2)}) copy-start(bf16[8,32,1024]{2,1,0:T(8,128)(2,1)S(1)} %collective-permute-done.13.refs_5_.rest_2_) | copy-start | bytes 1572868
  146.2 7.7 %copy-start.6 = (bf16[8,32,1024]{2,1,0:T(8,128)(2,1)}, bf16[8,32,1024]{2,1,0:T(8,128)(2,1)S(1)}, u32[]{:S(2)}) copy-start(bf16[8,32,1024]{2,1,0:T(8,128)(2,1)S(1)} %collective-permute-done.14.refs_6_.rest_3_) | copy-start | bytes 1572868
  150.8 0.9 copy-start.8
  151.7 14.3 %collective-permute-start.18 = (bf16[8,48,1024]{2,1,0:T(8,128)(2,1)}, bf16[8,48,1024]{2,1,0:T(8,128)(2,1)S(1)}, u32[]{:S(2)}, u32[]{:S(2)}) collective-permute-start(bf16[8,48,1024]{2,1,0:T(8,128)(2,1)} %get-tuple-element.60), channel_id=1, source_target_pairs={{0,8},{1,33},{2,10},{3,35},{4,12},{5,37},{6,14},{7,39},{8,16},{9,4... | collective-permute-start | bytes 2359304 | tf_op jit(solution)/shard_map/ppermute | solution.py:216
  151.9 31.1 %collective-permute-start.19 = (bf16[8,48,1024]{2,1,0:T(8,128)(2,1)}, bf16[8,48,1024]{2,1,0:T(8,128)(2,1)S(1)}, u32[]{:S(2)}, u32[]{:S(2)}) collective-permute-start(bf16[8,48,1024]{2,1,0:T(8,128)(2,1)} %get-tuple-element.61), channel_id=1, source_target_pairs={{0,16},{1,65},{2,18},{3,67},{4,20},{5,69},{6,22},{7,71},{8,24},{9,... | collective-permute-start | bytes 2359304 | tf_op jit(solution)/shard_map/ppermute | solution.py:216
  153.9 36.3 %collective-permute-start.20 = (bf16[8,48,1024]{2,1,0:T(8,128)(2,1)}, bf16[8,48,1024]{2,1,0:T(8,128)(2,1)}, u32[]{:S(2)}, u32[]{:S(2)}) collective-permute-start(bf16[8,48,1024]{2,1,0:T(8,128)(2,1)} %get-tuple-element.62), channel_id=1, source_target_pairs={{0,24},{1,97},{2,26},{3,99},{4,28},{5,101},{6,30},{7,103},{8,0},{9... | collective-permute-start | bytes 2359304 | tf_op jit(solution)/shard_map/ppermute | solution.py:216
  155.4 39.3 %copy-start.7 = (bf16[8,32,1024]{2,1,0:T(8,128)(2,1)S(1)}, bf16[8,32,1024]{2,1,0:T(8,128)(2,1)}, u32[]{:S(2)}) copy-start(bf16[8,32,1024]{2,1,0:T(8,128)(2,1)} %copy-done.6) | copy-start | bytes 1572868
  155.4 39.3 %copy-start.11 = (bf16[8,32,1024]{2,1,0:T(8,128)(2,1)S(1)}, bf16[8,32,1024]{2,1,0:T(8,128)(2,1)}, u32[]{:S(2)}) copy-start(bf16[8,32,1024]{2,1,0:T(8,128)(2,1)} %copy-done.10) | copy-start | bytes 1572868
  157.7 37.0 %copy-start.1 = (bf16[16,128,1024]{2,1,0:T(8,128)(2,1)S(1)}, bf16[16,128,1024]{2,1,0:T(8,128)(2,1)}, u32[]{:S(2)}) copy-start(bf16[16,128,1024]{2,1,0:T(8,128)(2,1)} %other_ref.5) | copy-start | bytes 12582916
  157.7 37.0 %copy-start.3 = (bf16[8,32,1024]{2,1,0:T(8,128)(2,1)S(1)}, bf16[8,32,1024]{2,1,0:T(8,128)(2,1)}, u32[]{:S(2)}) copy-start(bf16[8,32,1024]{2,1,0:T(8,128)(2,1)} %copy-done.2) | copy-start | bytes 1572868
  157.7 37.0 %copy-start.5 = (bf16[8,32,1024]{2,1,0:T(8,128)(2,1)S(1)}, bf16[8,32,1024]{2,1,0:T(8,128)(2,1)}, u32[]{:S(2)}) copy-start(bf16[8,32,1024]{2,1,0:T(8,128)(2,1)} %copy-done.4) | copy-start | bytes 1572868
  157.7 37.0 %copy-start.13 = (s32[32]{0:T(128)S(1)}, s32[32]{0:T(128)}, u32[]{:S(2)}) copy-start(s32[32]{0:T(128)} %find.1.ids_ref) | copy-start | bytes 388
  157.7 32.5 %collective-permute-start.15 = (bf16[8,48,1024]{2,1,0:T(8,128)(2,1)S(1)}, bf16[8,48,1024]{2,1,0:T(8,128)(2,1)S(1)}, u32[]{:S(2)}, u32[]{:S(2)}) collective-permute-start(bf16[8,48,1024]{2,1,0:T(8,128)(2,1)S(1)} %get-tuple-element.57), channel_id=1, source_target_pairs={{0,32},{1,9},{2,34},{3,11},{4,36},{5,13},{6,38},{7,15},{8,40},{9,1... | collective-permute-start | bytes 2359304 | tf_op jit(solution)/shard_map/ppermute | solution.py:216
  161.0 29.3 %collective-permute-start.16 = (bf16[8,48,1024]{2,1,0:T(8,128)(2,1)S(1)}, bf16[8,48,1024]{2,1,0:T(8,128)(2,1)S(1)}, u32[]{:S(2)}, u32[]{:S(2)}) collective-permute-start(bf16[8,48,1024]{2,1,0:T(8,128)(2,1)S(1)} %get-tuple-element.58), channel_id=1, source_target_pairs={{0,64},{1,17},{2,66},{3,19},{4,68},{5,21},{6,70},{7,23},{8,72},{9,... | collective-permute-start | bytes 2359304 | tf_op jit(solution)/shard_map/ppermute | solution.py:216
  166.0 25.1 %collective-permute-start.17 = (bf16[8,48,1024]{2,1,0:T(8,128)(2,1)S(1)}, bf16[8,48,1024]{2,1,0:T(8,128)(2,1)S(1)}, u32[]{:S(2)}, u32[]{:S(2)}) collective-permute-start(bf16[8,48,1024]{2,1,0:T(8,128)(2,1)S(1)} %get-tuple-element.59), channel_id=1, source_target_pairs={{0,96},{1,25},{2,98},{3,27},{4,100},{5,29},{6,102},{7,31},{8,104},... | collective-permute-start | bytes 2359304 | tf_op jit(solution)/shard_map/ppermute | solution.py:216
  191.2 12.1 %collective-permute-start.21 = (bf16[8,48,1024]{2,1,0:T(8,128)(2,1)S(1)}, bf16[8,48,1024]{2,1,0:T(8,128)(2,1)S(1)}, u32[]{:S(2)}, u32[]{:S(2)}) collective-permute-start(bf16[8,48,1024]{2,1,0:T(8,128)(2,1)S(1)} %get-tuple-element.64), channel_id=1, source_target_pairs={{0,8},{1,33},{2,10},{3,35},{4,12},{5,37},{6,14},{7,39},{8,16},{9,4... | collective-permute-start | bytes 2359304 | tf_op jit(solution)/shard_map/ppermute | solution.py:216
  193.1 19.8 %collective-permute-start.22 = (bf16[8,48,1024]{2,1,0:T(8,128)(2,1)S(1)}, bf16[8,48,1024]{2,1,0:T(8,128)(2,1)S(1)}, u32[]{:S(2)}, u32[]{:S(2)}) collective-permute-start(bf16[8,48,1024]{2,1,0:T(8,128)(2,1)S(1)} %get-tuple-element.65), channel_id=1, source_target_pairs={{0,16},{1,65},{2,18},{3,67},{4,20},{5,69},{6,22},{7,71},{8,24},{9,... | collective-permute-start | bytes 2359304 | tf_op jit(solution)/shard_map/ppermute | solution.py:216
  194.4 19.4 %collective-permute-start.23 = (bf16[8,48,1024]{2,1,0:T(8,128)(2,1)S(1)}, bf16[8,48,1024]{2,1,0:T(8,128)(2,1)S(1)}, u32[]{:S(2)}, u32[]{:S(2)}) collective-permute-start(bf16[8,48,1024]{2,1,0:T(8,128)(2,1)S(1)} %get-tuple-element.66), channel_id=1, source_target_pairs={{0,24},{1,97},{2,26},{3,99},{4,28},{5,101},{6,30},{7,103},{8,0},{9... | collective-permute-start | bytes 2359304 | tf_op jit(solution)/shard_map/ppermute | solution.py:216
  194.7 2.3 %copy-start.9 = (bf16[8,48,1024]{2,1,0:T(8,128)(2,1)S(1)}, bf16[8,48,1024]{2,1,0:T(8,128)(2,1)}, u32[]{:S(2)}) copy-start(bf16[8,48,1024]{2,1,0:T(8,128)(2,1)} %copy-done.8) | copy-start | bytes 2359300
